TPU v7x, 256 devices: a whole 4x4x8 slice. The times are simulated.
256 devices in a mesh: seq: 16 (over x, y), tp: 8 (over z), rep: 2 (over core).
Axes of the slice: x: 4, y: 4, z: 8, core: 2. Of those that a mesh axis runs over, the one named last changes fastest.
Arguments:
- prompt_x: bfloat16 [4, 8192, 16384], P('rep', 'seq', 'tp'), may hold values from -6 to 6
- prompt_bc: bfloat16 [4, 8192, 2, 8, 256], P('rep', 'seq', None, 'tp'), may hold values from -1.796875 to 1.796875
- prompt_dt: float32 [4, 8192, 256], P('rep', 'seq', 'tp'), may hold values from 0.3 to 3
- prompt_decay: float32 [4, 8192, 256], P('rep', 'seq', 'tp'), may hold values from -1.1 to 0
- lengths: int32 [4], P('rep'), may hold values from 256 to 8192, as said below
- owners: int32 [4], P('rep'), may hold values from 0 to 31, as said below
- gain: float32 [16384], P('tp'), may hold values from 0.5 to 1.5
- step_x: bfloat16 [32, 4, 16384], P(('seq', 'rep'), None, 'tp'), may hold values from -24 to 24
- step_bc: bfloat16 [32, 4, 2, 8, 256], P(('seq', 'rep'), None, None, 'tp'), may hold values from -1.796875 to 1.796875
- step_dt: float32 [32, 4, 256], P(('seq', 'rep'), None, 'tp'), may hold values from 0.3 to 3
- step_decay: float32 [32, 4, 256], P(('seq', 'rep'), None, 'tp'), may hold values from -0.7 to -0.02
Outputs:
- prefill_out: bfloat16 [4, 8192, 16384], P('rep', 'seq', 'tp')
- decode_out: bfloat16 [32, 4, 16384], P(('seq', 'rep'), None, 'tp')
Inputs may be any that keep to these rules, and one draw needn't show every extreme that they name: `lengths`: every length is a multiple of 256, and in every draw some prompt has length 8192. `owners`: no two prompts share a slot, and slots 0, 15 and 31 are taken in every draw. Slot o stands for seq index o // 2 and rep index o % 2.
All inputs are finite; a program needn't handle non-finite values.
Results may differ from a plain program's by a relative error of at most 0.0055.
Values sent between devices are 32-bit elements; how exact they have to be, the bound alone decides.
No kernel may reach another device: no remote copies, remote signals or barrier semaphores. Data moves between devices by JAX's collectives and lax.ppermute only.
A program may use at most 192 MiB of HBM per device.

v0:
```python
import jax
import jax.numpy as jnp
from jax import lax
from jax.sharding import PartitionSpec as P

STRETCH = 512


eps_norm = 1e-05


def prefix(array, axis, combine, identity):
    count, mine = (lax.axis_size(axis), lax.axis_index(axis))
    everything = jax.tree.map(lambda part: lax.all_gather(part, axis), array)
    start = jax.tree.map(
        lambda part, zero: jnp.broadcast_to(jnp.asarray(zero, part.dtype), part.shape),
        array,
        identity,
    )

    def lap(k, before):
        reached = k < mine
        new = combine(before, jax.tree.map(lambda part: part[k], everything))
        return jax.tree.map(lambda a, b: jnp.where(reached, a, b), new, before)

    return lax.fori_loop(0, count, lap, start)


def broadcast(array, axis, root):
    mine = lax.axis_index(axis) == root
    return lax.psum(jnp.where(mine, array, jnp.zeros_like(array)), axis)


def from_partner(value, axis, stride):
    mask = 2**stride
    pairs = [(source, source ^ mask) for source in range(lax.axis_size(axis))]
    return lax.ppermute(value, axis, pairs)


def local_block(x_block, bc_block, rate_block, gate_block):
    row_count, block_len, heads = rate_block.shape
    groups = bc_block.shape[3]
    per_group = heads // groups
    head_size = x_block.shape[2] // heads
    running = jnp.cumsum(gate_block, axis=1)
    run_heads = jnp.swapaxes(running, 1, 2)
    key_rows = bc_block[:, :, 0]
    scores = jnp.einsum(
        "rtgn,rsgn->rgts", bc_block[:, :, 1], key_rows, preferred_element_type=jnp.float32
    )
    scores = jnp.repeat(scores, per_group, axis=1)
    causal = jnp.tril(jnp.ones((block_len, block_len), dtype=jnp.bool_))
    gap_matrix = jnp.where(causal, run_heads[:, :, :, None] - run_heads[:, :, None, :], -jnp.inf)
    mixing = (scores * jnp.exp(gap_matrix) * jnp.swapaxes(rate_block, 1, 2)[:, :, None, :]).astype(
        jnp.bfloat16
    )
    values = x_block.reshape(row_count, block_len, heads, head_size)
    inner_term = jnp.einsum("rkts,rskp->rtkp", mixing, values, preferred_element_type=jnp.float32)
    tail_weight = jnp.exp(running[:, -1:, :] - running) * rate_block
    weighted = (values.astype(jnp.float32) * tail_weight[..., None]).astype(jnp.bfloat16)
    weighted = weighted.reshape(row_count, block_len, groups, per_group, head_size)
    block_state = jnp.einsum(
        "rsghp,rsgn->rghpn", weighted, key_rows, preferred_element_type=jnp.float32
    )
    return (inner_term, block_state.reshape(row_count, heads, head_size, -1), running)


def join_carry(earlier, later):
    return (earlier[0] + later[0], jnp.exp(later[0])[:, :, None, None] * earlier[1] + later[1])


def local(
    prompt_x,
    prompt_bc,
    prompt_dt,
    prompt_decay,
    lengths,
    owners,
    gain,
    step_x,
    step_bc,
    step_dt,
    step_decay,
):
    row_count, span, heads = prompt_dt.shape
    groups = prompt_bc.shape[3]
    per_group = heads // groups
    head_size = prompt_x.shape[2] // heads
    channels = heads * head_size * lax.axis_size("tp")
    seq_index = lax.axis_index("seq")
    positions = seq_index * span + jnp.arange(span, dtype=jnp.int32)
    in_prompt = (positions[None, :] < lengths[:, None]).astype(jnp.float32)
    gates = prompt_decay * in_prompt[:, :, None]
    rates = prompt_dt * in_prompt[:, :, None]
    local_state = jnp.zeros((row_count, heads, head_size, prompt_bc.shape[4]), jnp.float32)
    prefix_decay = jnp.zeros((row_count, heads), jnp.float32)
    inner_term, block_state, running = local_block(prompt_x, prompt_bc, rates, gates)
    local_before = local_state
    block_total = running[:, -1, :]
    local_state = jnp.exp(block_total)[:, :, None, None] * local_state + block_state
    incoming_decay, incoming = prefix(
        (block_total, local_state),
        "seq",
        join_carry,
        (jnp.zeros_like(block_total), jnp.zeros_like(local_state)),
    )
    before = jnp.exp(prefix_decay)[:, :, None, None] * incoming + local_before
    held_state = before.astype(jnp.bfloat16).reshape(row_count, groups, per_group, head_size, -1)
    outer_term = jnp.einsum(
        "rtgn,rghpn->rtghp",
        prompt_bc[:, 0:STRETCH, 1],
        held_state,
        preferred_element_type=jnp.float32,
    )
    outer_term = outer_term.reshape(row_count, STRETCH, heads, head_size)
    mixed = inner_term + jnp.exp(running)[..., None] * outer_term
    outputs = mixed.reshape(row_count, STRETCH, heads * head_size)
    mixed = outputs * in_prompt[:, :, None]
    squares = lax.psum(jnp.sum(mixed * mixed, axis=2), "tp")
    prefill_out = (mixed * lax.rsqrt(squares / channels + eps_norm)[:, :, None] * gain).astype(
        jnp.bfloat16
    )
    final_state = jnp.exp(block_total)[:, :, None, None] * incoming + local_state
    final_state = broadcast(final_state, "seq", lax.axis_size("seq") - 1)
    rep_index = lax.axis_index("rep")
    my_slot = seq_index * lax.axis_size("rep") + rep_index
    other_slot = seq_index * lax.axis_size("rep") + jnp.bitwise_xor(rep_index, 1)
    mine_flag = (owners == my_slot).astype(jnp.float32)
    other_flag = (owners == other_slot).astype(jnp.float32)
    own_state = jnp.sum(mine_flag[:, None, None, None] * final_state, axis=0)
    sent_state = jnp.sum(other_flag[:, None, None, None] * final_state, axis=0)
    got_state, got_flag = from_partner((sent_state, jnp.sum(other_flag)), "rep", 0)
    ssm_state = own_state + got_state
    filled = jnp.sum(mine_flag) + got_flag
    readings = []
    for step_index in range(step_x.shape[1]):
        key_heads = jnp.repeat(step_bc[0, step_index, 0].astype(jnp.float32), per_group, axis=0)
        query_heads = jnp.repeat(step_bc[0, step_index, 1].astype(jnp.float32), per_group, axis=0)
        step_vals = step_x[0, step_index].astype(jnp.float32).reshape(heads, head_size)
        ssm_state = (
            jnp.exp(step_decay[0, step_index])[:, None, None] * ssm_state
            + step_dt[0, step_index][:, None, None] * step_vals[:, :, None] * key_heads[:, None, :]
        )
        reading = jnp.einsum("kpn,kn->kp", ssm_state, query_heads, precision=lax.Precision.HIGHEST)
        readings.append(reading.reshape(heads * head_size))
    readings = jnp.stack(readings)
    step_squares = lax.psum(jnp.sum(readings * readings, axis=1), "tp")
    decode_out = readings * lax.rsqrt(step_squares / channels + eps_norm)[:, None] * gain * filled
    return (prefill_out, decode_out[None].astype(jnp.bfloat16))


def solution(mesh):
    in_specs = (
        P("rep", "seq", "tp"),
        P("rep", "seq", None, "tp", None),
        P("rep", "seq", "tp"),
        P("rep", "seq", "tp"),
        P("rep"),
        P("rep"),
        P("tp"),
        P(("seq", "rep"), None, "tp"),
        P(("seq", "rep"), None, None, "tp", None),
        P(("seq", "rep"), None, "tp"),
        P(("seq", "rep"), None, "tp"),
    )
    out_specs = (P("rep", "seq", "tp"), P(("seq", "rep"), None, "tp"))
    return jax.shard_map(local, mesh=mesh, in_specs=in_specs, out_specs=out_specs, check_vma=False)
```

profile of v0, /device:TPU:2, one launch (start us, length us, event | category | flops | bytes accessed | tf_op | source)
XLA Modules:
  0.0 686.4 jit_solution(13024668192585952305)
XLA Ops:
  16.1 6.2 copy.29
  29.2 23.3 %all-gather = f32[32,1,32]{2,1,0:T(1,128)S(1)} all-gather(f32[2,1,32]{2,1,0:T(1,128)S(1)} %copy.30), channel_id=2, replica_groups=mesh['seq'=16,'tp'=8,'rep'=2] {'seq'}, dimensions={0}, use_global_device_ids=true | all-gather | bytes 4352 | tf_op jit(solution)/shard_map/all_gather | solution.py:14
  52.5 352.1 %all-gather.4.cloned.1.call-done = f32[32,32,64,256]{3,2,1,0:T(8,128)} async-done(((f32[2,32,64,256]{3,2,1,0:T(8,128)}), f32[32,32,64,256]{3,2,1,0:T(8,128)}) %all-gather.4.cloned.1.call-update) | async-done | bytes 67108880 | tf_op jit(solution)/shard_map/all_gather | solution.py:14
  404.5 96.1 %while.14 = (s32[]{:T(128)}, f32[2,32,64,256]{3,2,1,0:T(8,128)}, s32[]{:T(128)}, f32[16,2,32]{2,1,0:T(2,128)S(1)}, f32[16,2,32,64,256]{4,3,2,1,0:T(8,128)}, /*index=5*/s32[]{:T(128)}, s32[]{:T(128)}) while((s32[]{:T(128)}, f32[2,32,64,256]{3,2,1,0:T(8,128)}, s32[]{:T(128)}, f32[16,2,32]{2,1,0:T(2,128)S(1)}, ...), condition=%wide.region_3.4_spmd.clone, body=%wide.region_2.3_spmd.clone.sunk | while | flops 4194308 | bytes 12583785 | solution.py:26
  409.4 6.1 fusion.59
  415.4 6.1 fusion.59
  421.5 6.1 fusion.59
  427.6 6.1 fusion.59
  433.7 6.1 fusion.59
  439.8 6.1 fusion.59
  445.9 6.1 fusion.59
  451.9 6.1 fusion.59
  458.0 6.1 fusion.59
  464.1 6.1 fusion.59
  470.2 6.1 fusion.59
  476.3 6.1 fusion.59
  482.4 6.1 fusion.59
  488.5 6.1 fusion.59
  494.5 6.1 fusion.59
  508.2 23.9 %fusion.1 = f32[2,32,512,64]{2,3,1,0:T(8,128)} fusion(bf16[2,512,32,64]{1,3,2,0:T(8,128)(2,1)} %bitcast.104, f32[2,32,512]{2,1,0:T(8,128)S(1)} %get-tuple-element.140, f32[2,32,512]{2,1,0:T(8,128)S(1)} %get-tuple-element.145, f32[2,512,512]{2,1,0:T(8,128)S(1)} %fusion.34, pred[512,512]{1,0:T(8,128)(4,1)S(1)} %iota_compare_fusion), kind=kOutput, calls=%fused_computation.4 | convolution fusion | flops 2231369728 | bytes 15204352 | tf_op jit(solution)/shard_map/rkts,rskp->rtkp/dot_general | solution.py:58
  532.1 88.0 %all-reduce.3.cloned.1.call-done = f32[2,32,64,256]{3,2,1,0:T(8,128)} async-done(((f32[2,32,64,256]{3,2,1,0:T(8,128)}), f32[2,32,64,256]{3,2,1,0:T(8,128)}) %all-reduce.3.cloned.1.call-update) | async-done | bytes 4194320 | tf_op jit(solution)/shard_map/psum | solution.py:31
  626.4 7.8 %multiply_reduce_fusion = (f32[2,512]{1,0:T(2,128)S(1)}, f32[2,512,32,64]{1,3,2,0:T(8,128)}) fusion(f32[2,512]{1,0:T(2,128)S(1)} %compare_convert_fusion, bf16[2,512,1,1,256]{4,2,3,1,0:T(2,128)(2,1)S(1)} %get-tuple-element.137, f32[2,32,64,256]{3,2,1,0:T(8,128)} %get-tuple-element.96, f32[2,512,32]{1,2,0:T(8,128)S(1)} %get-tuple-element.141, ...), kind=kOutput, calls=%fused_computation.9 | convolution fusion | flops 1085275136 | bytes 21635072 | tf_op jit(solution)/shard_map/rtgn,rghpn->rtghp/dot_general | solution.py:109
  634.3 8.7 %copy.31 = f32[2,512,2048]{2,1,0:T(8,128)} copy(f32[2,512,2048]{1,2,0:T(8,128)} %bitcast.102) | data formatting | bytes 16777216 | tf_op jit(solution)/shard_map/reshape | solution.py:117
  655.7 17.7 %all-reduce = (f32[2,512]{1,0:T(2,128)S(1)}, f32[4]{0:T(128)S(1)}) all-reduce(f32[2,512]{1,0:T(2,128)S(1)} %get-tuple-element.166, f32[4]{0:T(128)S(1)} %fusion.44), channel_id=1, replica_groups=mesh['seq'=16,'tp'=8,'rep'=2] {'tp'}, use_global_device_ids=true, to_apply=%region_5.6 | all-reduce | flops 1028 | bytes 8224 | tf_op jit(solution)/shard_map/psum | solution.py:119
  (86 shorter events, 52.0 us)
Async XLA Ops:
  7.2 397.4 %all-gather.4.cloned.1.call-start = ((), (), s32[]{:S(2)}) async-start(), calls=%async_computation.1 | async-start | bytes 71303168 | tf_op jit(solution)/shard_map/all_gather | solution.py:14
  27.8 0.7 copy-start.5
  27.8 592.3 %all-reduce.3.cloned.1.call-start = ((), (), s32[]{:S(2)}) async-start(), calls=%async_computation | async-start | bytes 8388608 | tf_op jit(solution)/shard_map/psum | solution.py:31
  29.1 596.1 %collective-permute-start.1 = (f32[]{:T(128)}, f32[]{:T(128)}, u32[]{:S(2)}, u32[]{:S(2)}) collective-permute-start(f32[]{:T(128)} %get-tuple-element.164), channel_id=1, source_target_pairs={{0,1},{1,0},{2,3},{3,2},{4,5},{5,4},{6,7},{7,6},{8,9},{9,8},{10,11... | collective-permute-start | bytes 20 | tf_op jit(solution)/shard_map/ppermute | solution.py:37
  506.5 0.7 copy-start
  620.1 4.8 copy-start.3
  620.1 4.8 copy-start.4
  620.1 4.9 copy-start.2
  624.9 18.0 %collective-permute-start = (f32[32,64,256]{2,1,0:T(8,128)S(1)}, f32[32,64,256]{2,1,0:T(8,128)}, u32[]{:S(2)}, u32[]{:S(2)}) collective-permute-start(f32[32,64,256]{2,1,0:T(8,128)S(1)} %get-tuple-element.115), channel_id=1, source_target_pairs={{0,1},{1,0},{2,3},{3,2},{4,5},{5,4},{6,7},{7,6},{8,9},{9,8},{10,11... | collective-permute-start | bytes 6291464 | tf_op jit(solution)/shard_map/ppermute | solution.py:37
  648.3 25.2 %copy-start.1 = (f32[2048]{0:T(1024)S(1)}, f32[2048]{0:T(1024)}, u32[]{:S(2)}) copy-start(f32[2048]{0:T(1024)} %param.19) | copy-start | bytes 24580
Sparse Core Ops, SparseCore 0:
  27.9 376.5 all-gather.3
  506.6 113.4 all-reduce.2
where the time goes:
time: 687 us; the launch traced here: 686 us
  waiting for transfers between devices  440 us (64%)
  other arithmetic  122 us (18%)
  matrix products  46.9 us (7%)
  blocking collectives  41 us (6%)
  local copies, waits for them, and re-layouts  21 us (3%)
  between operations  15.4 us (2%)
    all_gather x1, waiting for transfers between devices, prefix(): everything = jax.tree.map(lambda part: lax.all_gather(part, axis), array)  352 us
    select_n x16, other arithmetic, lap(): return jax.tree.map(lambda a, b: jnp.where(reached, a, b), new, before)  96 us
    psum x1, waiting for transfers between devices, broadcast(): return lax.psum(jnp.where(mine, array, jnp.zeros_like(array)), axis)  88 us
    dot_general x1, matrix products, local_block(): jnp.einsum('rkts,rskp->rtkp', mixing, values, preferred_element_type=jnp....  23.9 us
    all_gather x1, blocking collectives, prefix(): everything = jax.tree.map(lambda part: lax.all_gather(part, axis), array)  23.3 us
    psum x1, blocking collectives, local(): squares = lax.psum(jnp.sum(mixed * mixed, axis=2), 'tp')  17.7 us
  transfers between devices with their start and end apart: 4, of which 2 were waited for; matrix products, arithmetic and copies ran while one was open for 22% of the time, Pallas kernels for 0%

commit v1 on v0

v1 whole, which is shorter than its diff:
```python
import functools

import jax
import jax.numpy as jnp
from jax import lax
from jax.experimental import pallas as pl
from jax.experimental.pallas import tpu as pltpu
from jax.sharding import PartitionSpec as P

eps_norm = 1e-05
TILE = 512
SUB = 128
HIGH = lax.Precision.HIGHEST
F32 = jnp.float32
BF16 = jnp.bfloat16


def remaining(lengths_ref, row, span):
    return lengths_ref[row] - lax.axis_index("seq") * span


def params(semantics, mib):
    return pltpu.CompilerParams(dimension_semantics=semantics, vmem_limit_bytes=mib * 2**20)


def split3(value):
    first = value.astype(BF16)
    rest = value - first.astype(F32)
    second = rest.astype(BF16)
    third = (rest - second.astype(F32)).astype(BF16)
    return jnp.concatenate([first, second, third], axis=0)


def head_columns(heads, head_size, start, width):
    row = lax.broadcasted_iota(jnp.int32, (3 * heads, width), 0)
    col = lax.broadcasted_iota(jnp.int32, (3 * heads, width), 1) + start
    return (lax.rem(row, heads) == col // head_size).astype(BF16)


def spread(parts, columns):
    return lax.dot_general(parts, columns, (((0,), (0,)), ((), ())), preferred_element_type=F32)


def prepare_kernel(lengths_ref, decay_ref, dt_ref, bc_ref, run_ref, tail_ref, end_ref, b_ref, c_ref):
    row = pl.program_id(0)
    heads, span = decay_ref.shape[1], decay_ref.shape[2]
    here = lax.broadcasted_iota(jnp.int32, (heads, span), 1) < remaining(lengths_ref, row, span)
    gates = jnp.where(here, decay_ref[0], 0.0)
    rates = jnp.where(here, dt_ref[0], 0.0)
    upto = (
        lax.broadcasted_iota(jnp.int32, (span, span), 0)
        <= lax.broadcasted_iota(jnp.int32, (span, span), 1)
    ).astype(BF16)
    sums = jnp.dot(split3(gates), upto, preferred_element_type=F32)
    running = sums[:heads] + sums[heads : 2 * heads] + sums[2 * heads :]
    run_ref[0] = running
    total = running[:, span - 1 : span]
    tail_ref[0] = split3(jnp.exp(total - running) * rates).T
    end_ref[0] = split3(jnp.broadcast_to(jnp.exp(total), (heads, SUB))).T[:16]
    b_ref[0] = bc_ref[0, :, 0, :].T
    c_ref[0] = bc_ref[0, :, 1, :]


def pre_kernel(head_size, owners_ref, tail_ref, end_ref, b_ref, query_ref, other_ref, x_ref, out_ref, keys_ref):
    tile, row = pl.program_id(0), pl.program_id(1)

    @pl.when(jnp.logical_and(tile == 0, row == 0))
    def _():
        chip = lax.axis_index("seq") * 2
        rep = lax.axis_index("rep")
        for prompt in range(2):
            mine = jnp.where(owners_ref[prompt] == chip + rep, 1.0, 0.0)
            other = jnp.where(owners_ref[prompt] == chip + 1 - rep, 1.0, 0.0)
            chosen = mine * query_ref[...] + other * other_ref[...]
            for half in range(2):
                keys_ref[8 * half + 4 * prompt : 8 * half + 4 * prompt + 4, :] = chosen[:, half * SUB : (half + 1) * SUB]

    heads, width, states = tail_ref.shape[2] // 3, x_ref.shape[2], b_ref.shape[1]
    columns = head_columns(heads, head_size, tile * width, width)
    weights = jnp.dot(tail_ref[row], columns, preferred_element_type=F32)
    weighted = (x_ref[0].astype(F32) * weights).astype(BF16)
    state = jnp.dot(b_ref[row], weighted, preferred_element_type=F32)
    ends = jnp.dot(end_ref[row], columns, preferred_element_type=F32)
    for chunk in range(out_ref.shape[0]):
        lanes = slice(chunk * SUB, (chunk + 1) * SUB)
        out_ref[chunk, pl.ds(pl.multiple_of(row * states, states), states), :] = state[:, lanes]
        out_ref[chunk, pl.ds(2 * states + row, 1), :] = ends[:1, lanes]

        @pl.when(row == 0)
        def _():
            out_ref[chunk, 2 * states + 8 :, :] = keys_ref[...]


def scan_kernel(in_ref, out_ref, carry_ref, key_ref, held_ref, sems):
    step = pl.program_id(0)
    count, states = in_ref.shape[0], 256

    @pl.when(step == 0)
    def _():
        carry_ref[...] = jnp.zeros_like(carry_ref)
        key_ref[...] = jnp.zeros_like(key_ref)

    for part in range(count):
        for row in range(2):
            rows = slice(row * states, (row + 1) * states)
            before = carry_ref[rows, :]
            held_ref[step * count + part, rows, :] = before
            carry_ref[rows, :] = (
                in_ref[part, 2 * states + row : 2 * states + row + 1, :] * before + in_ref[part, rows, :]
            )
        key_ref[...] += in_ref[part, 2 * states + 8 :, :]

    def send(k):
        parts = pl.ds(k * count, count)
        rows = pl.ds(0, 2 * states)
        return pltpu.make_async_copy(held_ref.at[parts, rows, :], out_ref.at[parts, rows, :], sems.at[k])

    send(step).start()

    @pl.when(step == pl.num_programs(0) - 1)
    def _():
        first, second = key_ref[:8, :], key_ref[8:, :]
        answers = []
        for row in range(2):
            upper = carry_ref[row * states : row * states + 128, :]
            lower = carry_ref[row * states + 128 : (row + 1) * states, :]
            answer = jnp.dot(first, upper, precision=HIGH, preferred_element_type=F32)
            answers.append(answer + jnp.dot(second, lower, precision=HIGH, preferred_element_type=F32))
        pick = lax.broadcasted_iota(jnp.int32, (8, 128), 0) < 4
        both = jnp.where(pick, answers[0], answers[1])
        total = held_ref.shape[0]
        for part in range(total):
            held_ref[part, 2 * states :, :] = both
        rest = pl.ds(2 * states, 8)
        last = pltpu.make_async_copy(held_ref.at[:, rest, :], out_ref.at[:, rest, :], sems.at[total // count])
        last.start()
        for k in range(total // count):
            send(k).wait()
        last.wait()


def inner_kernel(head_size, lengths_ref, run_ref, dt_ref, b_ref, c_ref, x_ref, out_ref, grow_ref, scores_ref, near_ref, mid_ref, far_ref, own_ref, other_ref):
    row, tile = pl.program_id(0), pl.program_id(1)
    heads, span = run_ref.shape[1], run_ref.shape[2]
    width = x_ref.shape[2]

    @pl.when(tile == 0)
    def _():
        running = run_ref[0]
        here = lax.broadcasted_iota(jnp.int32, (heads, span), 1) < remaining(lengths_ref, row, span)
        rates = jnp.where(here, dt_ref[0], 0.0)
        scores = jnp.dot(c_ref[0], b_ref[0], preferred_element_type=F32)
        causal = lax.broadcasted_iota(jnp.int32, (span, span), 0) >= lax.broadcasted_iota(
            jnp.int32, (span, span), 1
        )
        scores_ref[...] = jnp.where(causal, scores, 0.0).astype(BF16)

        def at(index):
            return running[:, index : index + 1]

        def blocks(references, start=0):
            return jnp.concatenate(
                [
                    jnp.broadcast_to(reference, (heads, SUB))
                    for reference in references
                ],
                axis=1,
            )

        middles = blocks([at(k * SUB + SUB // 2 - 1) for k in range(4)])
        near_ref[...] = split3(jnp.exp(middles - running) * rates)
        own_ref[...] = split3(jnp.where(here, jnp.exp(running - middles), 0.0))
        ends = blocks([at(SUB - 1), at(SUB - 1), at(3 * SUB - 1), at(3 * SUB - 1)])
        mid_ref[...] = split3(jnp.exp(jnp.minimum(ends - running, 0.0)) * rates)
        halves = jnp.broadcast_to(at(2 * SUB - 1), (heads, span))
        far_ref[...] = split3(jnp.exp(jnp.minimum(halves - running, 0.0)) * rates)
        starts = blocks([at(0), at(SUB - 1), at(2 * SUB - 1), at(3 * SUB - 1)])
        other_ref[...] = split3(jnp.where(here, jnp.exp(jnp.minimum(running - starts, 0.0)), 0.0))
        grow_ref[0] = split3(jnp.where(here, jnp.exp(running), 0.0)).T

    columns = head_columns(heads, head_size, tile * width, width)
    values = x_ref[0].astype(F32)

    def part(k, n=1):
        return slice(k * SUB, (k + n) * SUB)

    def weigh(parts, rows):
        return (values[rows] * spread(parts[:, rows], columns)).astype(BF16)

    def apply(rows, cols, weighted):
        return jnp.dot(scores_ref[rows, cols], weighted, preferred_element_type=F32)

    far = apply(part(2, 2), part(0, 2), weigh(far_ref, part(0, 2)))
    mids = [apply(part(1), part(0), weigh(mid_ref, part(0))), apply(part(3), part(2), weigh(mid_ref, part(2)))]
    running = run_ref[0]
    gap = jnp.exp(running[:, 3 * SUB - 1 : 3 * SUB] - running[:, 2 * SUB - 1 : 2 * SUB])
    gap = spread(split3(jnp.broadcast_to(gap, (heads, SUB))), columns)
    others = [None, mids[0], far[:SUB], mids[1] + gap * far[SUB:]]
    for k in range(4):
        near = apply(part(k), part(k), weigh(near_ref, part(k)))
        result = spread(own_ref[:, part(k)], columns) * near
        if others[k] is not None:
            result = result + spread(other_ref[:, part(k)], columns) * others[k]
        out_ref[0, part(k), :] = result.astype(BF16)


def post_kernel(head_size, grow_ref, c_ref, held_ref, inner_ref, out_ref, square_ref, total_ref):
    row, tile = pl.program_id(0), pl.program_id(1)
    heads = grow_ref.shape[2] // 3
    width = inner_ref.shape[2]

    @pl.when(tile == 0)
    def _():
        total_ref[...] = jnp.zeros_like(total_ref)

    columns = head_columns(heads, head_size, tile * width, width)
    held = jnp.concatenate([held_ref[k].astype(BF16) for k in range(held_ref.shape[0])], axis=1)
    outer = jnp.dot(c_ref[0], held, preferred_element_type=F32)
    grow = jnp.dot(grow_ref[0], columns, preferred_element_type=F32)
    mixed = inner_ref[0].astype(F32) + grow * outer
    out_ref[0] = mixed.astype(BF16)
    squares = mixed * mixed
    partial = total_ref[...]
    for k in range(width // SUB):
        partial += squares[:, k * SUB : (k + 1) * SUB]
    total_ref[...] = partial

    @pl.when(tile == pl.num_programs(1) - 1)
    def _():
        square_ref[0] = lax.dot_general(
            jnp.ones((8, SUB), F32),
            partial,
            (((1,), (1,)), ((), ())),
            precision=HIGH,
            preferred_element_type=F32,
        )


def decode_kernel(head_size, square_ref, mine_ref, own_ref, got_ref, factor_ref, x_ref, reading_ref, sums_ref):
    steps, width = x_ref.shape
    heads = factor_ref.shape[1]
    columns = head_columns(heads, head_size, 0, width)
    factors = spread(split3(factor_ref[...].T), columns)
    answers = own_ref[...]
    start = got_ref[:steps, :]
    for prompt in range(2):
        start = start + mine_ref[prompt] * answers[prompt * steps : (prompt + 1) * steps]
    values = x_ref[...].astype(F32)
    readings = factors[:steps] * start
    for j in range(steps):
        readings = readings + factors[(j + 1) * steps : (j + 2) * steps] * values[j : j + 1]
    reading_ref[...] = readings
    squares = jnp.broadcast_to(jnp.sum(readings * readings, axis=1, keepdims=True), (steps, SUB))
    blocks = square_ref.shape[2] // SUB
    for part in range(sums_ref.shape[0]):
        for row in range(2):
            for k in range(blocks):
                sums_ref[part, row * blocks + k : row * blocks + k + 1, :] = square_ref[row, :1, k * SUB : (k + 1) * SUB]
        sums_ref[part, 2 * blocks :, :] = squares


def final_kernel(channels, sums_ref, gain_ref, filled_ref, reading_ref, mixed_ref, out_ref, step_ref):
    row = pl.program_id(0)
    sums = jnp.sum(sums_ref[...], axis=0)
    scales = lax.rsqrt(sums / channels + eps_norm)
    gain = gain_ref[...]
    span = mixed_ref.shape[1]
    count = span // SUB
    mine = jnp.where(row == 0, scales[:count], scales[count : 2 * count])
    columns = jnp.concatenate([mine, mine], axis=0).T
    for k in range(count):
        rows = slice(k * SUB, (k + 1) * SUB)
        out_ref[0, rows, :] = (mixed_ref[0, rows, :].astype(F32) * columns[:, k : k + 1] * gain).astype(BF16)

    @pl.when(row == 0)
    def _():
        scale = scales[2 * count :, :1]
        step_ref[...] = (reading_ref[...] * scale * gain * filled_ref[0]).astype(BF16)


def local(prompt_x, prompt_bc, prompt_dt, prompt_decay, lengths, owners, gain, step_x, step_bc, step_dt, step_decay):
    rows, span, heads = prompt_dt.shape
    width = prompt_x.shape[2]
    head_size = width // heads
    states = prompt_bc.shape[4]
    steps = step_x.shape[1]
    channels = width * lax.axis_size("tp")
    seq_count = lax.axis_size("seq")
    seq_index, rep_index = lax.axis_index("seq"), lax.axis_index("rep")
    decay_t = jnp.swapaxes(prompt_decay, 1, 2)
    dt_t = jnp.swapaxes(prompt_dt, 1, 2)
    tiles = width // TILE
    per_tile = TILE // SUB
    smem = pl.BlockSpec(memory_space=pltpu.SMEM)

    my_slot = seq_index * 2 + rep_index
    other_slot = seq_index * 2 + 1 - rep_index
    queries = step_bc[0, :, 1, 0].astype(F32)
    swap = [(0, 1), (1, 0)]
    other_queries = lax.ppermute(queries, "rep", swap)
    mine = (owners == my_slot).astype(F32)
    other = (owners == other_slot).astype(F32)
    key_rows = 2 * rows * steps
    sent_rows = rows * states + 8 + key_rows
    bc = jnp.swapaxes(prompt_bc, 2, 3)[:, :, 0]
    per_row = lambda *dims: pl.BlockSpec((1,) + dims, lambda r: (r,) + (0,) * len(dims))
    whole = lambda *dims: pl.BlockSpec(dims, lambda *_: (0,) * len(dims))
    running, tails, ends, b_rows, c_rows = pl.pallas_call(
        prepare_kernel,
        grid=(rows,),
        in_specs=[smem, per_row(heads, span), per_row(heads, span), per_row(span, 2, states)],
        out_specs=[
            per_row(heads, span),
            per_row(span, 3 * heads),
            per_row(16, 3 * heads),
            per_row(states, span),
            per_row(span, states),
        ],
        out_shape=[
            jax.ShapeDtypeStruct((rows, heads, span), F32),
            jax.ShapeDtypeStruct((rows, span, 3 * heads), BF16),
            jax.ShapeDtypeStruct((rows, 16, 3 * heads), BF16),
            jax.ShapeDtypeStruct((rows, states, span), BF16),
            jax.ShapeDtypeStruct((rows, span, states), BF16),
        ],
        compiler_params=params(("arbitrary",), 60),
        name="prepare",
    )(lengths, decay_t, dt_t, bc)

    big = 1024
    sent = pl.pallas_call(
        functools.partial(pre_kernel, head_size),
        grid=(width // big, rows),
        in_specs=[
            smem,
            whole(rows, span, 3 * heads),
            whole(rows, 16, 3 * heads),
            whole(rows, states, span),
            whole(steps, states),
            whole(steps, states),
            pl.BlockSpec((1, span, big), lambda j, r: (r, 0, j)),
        ],
        out_specs=pl.BlockSpec((big // SUB, sent_rows, SUB), lambda j, r: (j, 0, 0)),
        out_shape=jax.ShapeDtypeStruct((width // SUB, sent_rows, SUB), F32),
        scratch_shapes=[pltpu.VMEM((key_rows, SUB), F32)],
        compiler_params=params(("arbitrary", "arbitrary"), 60),
        name="block_states",
    )(owners, tails, ends, b_rows, queries, other_queries, prompt_x)

    got = lax.all_to_all(sent, "seq", 0, 0)

    per_step = 4
    back_rows = rows * states + 8
    back = pl.pallas_call(
        scan_kernel,
        grid=(seq_count // per_step,),
        in_specs=[pl.BlockSpec((per_step, sent_rows, SUB), lambda k: (k, 0, 0))],
        out_specs=pl.BlockSpec(memory_space=pl.ANY),
        out_shape=jax.ShapeDtypeStruct((seq_count, back_rows, SUB), F32),
        scratch_shapes=[
            pltpu.VMEM((rows * states, SUB), F32),
            pltpu.VMEM((key_rows, SUB), F32),
            pltpu.VMEM((seq_count, back_rows, SUB), F32),
            pltpu.SemaphoreType.DMA((seq_count // per_step + 1,)),
        ],
        compiler_params=params(("arbitrary",), 60),
        name="prefix_states",
    )(got)

    held = lax.all_to_all(back, "seq", 0, 0)

    inner, grows = pl.pallas_call(
        functools.partial(inner_kernel, head_size),
        grid=(rows, tiles),
        in_specs=[
            smem,
            pl.BlockSpec((1, heads, span), lambda r, j: (r, 0, 0)),
            pl.BlockSpec((1, heads, span), lambda r, j: (r, 0, 0)),
            pl.BlockSpec((1, states, span), lambda r, j: (r, 0, 0)),
            pl.BlockSpec((1, span, states), lambda r, j: (r, 0, 0)),
            pl.BlockSpec((1, span, TILE), lambda r, j: (r, 0, j)),
        ],
        out_specs=[
            pl.BlockSpec((1, span, TILE), lambda r, j: (r, 0, j)),
            pl.BlockSpec((1, span, 3 * heads), lambda r, j: (r, 0, 0)),
        ],
        out_shape=[
            jax.ShapeDtypeStruct((rows, span, width), BF16),
            jax.ShapeDtypeStruct((rows, span, 3 * heads), BF16),
        ],
        scratch_shapes=[pltpu.VMEM((span, span), BF16)] + [pltpu.VMEM((3 * heads, span), BF16)] * 5,
        compiler_params=params(("arbitrary", "arbitrary"), 60),
        cost_estimate=pl.CostEstimate(flops=20 * 10**9, bytes_accessed=32 * 2**20, transcendentals=10**6),
        name="inner_terms",
    )(lengths, running, dt_t, b_rows, c_rows, prompt_x)

    answers = held[:, rows * states :, :].transpose(1, 0, 2).reshape(rows * steps, width)
    sent_answer = jnp.sum(other[:, None, None] * answers.reshape(rows, steps, width), axis=0)
    flags = jnp.broadcast_to(jnp.sum(other), (8 - steps, width))
    sent_answer, inner = lax.optimization_barrier((jnp.concatenate([sent_answer, flags], axis=0), inner))
    got_answer = lax.ppermute(sent_answer, "rep", swap)

    big = 1024
    mixed, squares = pl.pallas_call(
        functools.partial(post_kernel, head_size),
        grid=(rows, width // big),
        in_specs=[
            pl.BlockSpec((1, span, 3 * heads), lambda r, j: (r, 0, 0)),
            pl.BlockSpec((1, span, states), lambda r, j: (r, 0, 0)),
            pl.BlockSpec((big // SUB, states, SUB), lambda r, j: (j, r, 0)),
            pl.BlockSpec((1, span, big), lambda r, j: (r, 0, j)),
        ],
        out_specs=[
            pl.BlockSpec((1, span, big), lambda r, j: (r, 0, j)),
            pl.BlockSpec((1, 8, span), lambda r, j: (r, 0, 0)),
        ],
        out_shape=[
            jax.ShapeDtypeStruct((rows, span, width), BF16),
            jax.ShapeDtypeStruct((rows, 8, span), F32),
        ],
        scratch_shapes=[pltpu.VMEM((span, SUB), F32)],
        compiler_params=params(("arbitrary", "arbitrary"), 60),
        cost_estimate=pl.CostEstimate(flops=4 * 10**9, bytes_accessed=12 * 2**20, transcendentals=0),
        name="outer_terms",
    )(grows, c_rows, held, inner)

    keys_step = step_bc[0, :, 0, 0].astype(F32)
    sums = jnp.cumsum(step_decay[0], axis=0)
    products = jnp.einsum("jn,kn->jk", keys_step, queries, precision=HIGH)
    later = jnp.arange(steps)[:, None] <= jnp.arange(steps)[None, :]
    gaps = jnp.where(later[:, :, None], sums[None, :, :] - sums[:, None, :], -jnp.inf)
    factors = jnp.exp(gaps) * step_dt[0][:, None] * products[:, :, None]
    factors = jnp.concatenate([jnp.exp(sums)[None], factors], axis=0).reshape((steps + 1) * steps, heads)
    factors = jnp.pad(factors, ((0, 24 - factors.shape[0]), (0, 0)))
    tp_count = lax.axis_size("tp")
    readings, partial = pl.pallas_call(
        functools.partial(decode_kernel, head_size),
        in_specs=[
            pl.BlockSpec(memory_space=pltpu.VMEM),
            smem,
        ] + [pl.BlockSpec(memory_space=pltpu.VMEM)] * 4,
        out_shape=[
            jax.ShapeDtypeStruct((steps, width), F32),
            jax.ShapeDtypeStruct((tp_count, rows * span // SUB + steps, SUB), F32),
        ],
        name="decode",
    )(squares, mine, answers, got_answer, factors, step_x[0])
    filled = (jnp.sum(mine) + got_answer[steps, 0])
    gathered = lax.all_to_all(partial, "tp", 0, 0)
    prefill_out, decode_out = pl.pallas_call(
        functools.partial(final_kernel, float(channels)),
        grid=(rows, 2),
        in_specs=[
            whole(*gathered.shape),
            pl.BlockSpec((1, width // 2), lambda r, j: (0, j)),
            smem,
            pl.BlockSpec((steps, width // 2), lambda r, j: (0, j)),
            pl.BlockSpec((1, span, width // 2), lambda r, j: (r, 0, j)),
        ],
        out_specs=[
            pl.BlockSpec((1, span, width // 2), lambda r, j: (r, 0, j)),
            pl.BlockSpec((steps, width // 2), lambda r, j: (0, jnp.where(r == 0, j, 1))),
        ],
        out_shape=[
            jax.ShapeDtypeStruct((rows, span, width), BF16),
            jax.ShapeDtypeStruct((steps, width), BF16),
        ],
        compiler_params=params(("arbitrary", "arbitrary"), 60),
        name="normalize",
    )(gathered, gain[None], filled[None], readings, mixed)
    return (prefill_out, decode_out[None])


def solution(mesh):
    in_specs = (
        P("rep", "seq", "tp"),
        P("rep", "seq", None, "tp", None),
        P("rep", "seq", "tp"),
        P("rep", "seq", "tp"),
        P("rep"),
        P("rep"),
        P("tp"),
        P(("seq", "rep"), None, "tp"),
        P(("seq", "rep"), None, None, "tp", None),
        P(("seq", "rep"), None, "tp"),
        P(("seq", "rep"), None, "tp"),
    )
    out_specs = (P("rep", "seq", "tp"), P(("seq", "rep"), None, "tp"))
    return jax.shard_map(local, mesh=mesh, in_specs=in_specs, out_specs=out_specs, check_vma=False)
```

time: 687 us -> 182 us (0.26)
  the two profiles are of different devices: /device:TPU:2 before, /device:TPU:28 now
where the time goes in v1:
time: 182 us; the launch traced here: 181 us
  blocking collectives  56.8 us (31%)
  Pallas kernels  51.4 us (28%)
  waiting for transfers between devices  45.9 us (25%)
  starting transfers between devices  16.9 us (9%)
  local copies, waits for them, and re-layouts  6.62 us (4%)
  between operations  2 us (1%)
    all_to_all x1, blocking collectives, local(): got = lax.all_to_all(sent, 'seq', 0, 0)  56.8 us
    all_to_all x1, waiting for transfers between devices, local(): held = lax.all_to_all(back, 'seq', 0, 0)  40 us
    pallas_call x1, Pallas kernels, local(): pl.pallas_call(functools.partial(inner_kernel, head_size), grid=(rows, ti...  18.5 us
    all_to_all x1, starting transfers between devices, local(): held = lax.all_to_all(back, 'seq', 0, 0)  8.41 us
    all_to_all x1, starting transfers between devices, local(): gathered = lax.all_to_all(partial, 'tp', 0, 0)  8.32 us
    pallas_call x1, Pallas kernels, local(): pl.pallas_call(functools.partial(post_kernel, head_size), grid=(rows, wid...  8.08 us
    pallas_call x1, Pallas kernels, local(): pl.pallas_call(functools.partial(pre_kernel, head_size), grid=(width // b...  7.43 us
    all_to_all x1, waiting for transfers between devices, local(): gathered = lax.all_to_all(partial, 'tp', 0, 0)  5.95 us
  transfers between devices with their start and end apart: 4, of which 2 were waited for; matrix products, arithmetic and copies ran while one was open for 2% of the time, Pallas kernels for 17%

profile of v1, /device:TPU:28, one launch (start us, length us, event | category | flops | bytes accessed | tf_op | source)
XLA Modules:
  0.0 181.2 jit_solution(4320495515117714653)
XLA Ops:
  0.6 0.8 fusion.6
  1.4 0.1 collective-permute-start
  1.5 4.9 %prepare.1 = (f32[2,32,512]{2,1,0:T(8,128)}, bf16[2,512,96]{2,1,0:T(8,128)(2,1)}, bf16[2,16,96]{2,1,0:T(8,128)(2,1)}, bf16[2,256,512]{2,1,0:T(8,128)(2,1)}, bf16[2,512,256]{2,1,0:T(8,128)(2,1)}) custom-call(s32[2]{0:T(128)} %lengths_ref.3, f32[2,32,512]{2,1,0:T(8,128)} %bitcast.26, f32[2,32,512]{2,1,0:T(8,128)} %bitcast.27, bf16[2,512,2,256]{3,2,1,0:T(2,128)(2,1)} %bitcast.25), custom_call_target="tpu_custom_call" | custom-call | tf_op jit(solution)/shard_map/prepare/pallas_call | solution.py:308
  6.5 0.6 copy-done.3
  7.1 7.4 %block_states.1 = f32[16,536,128]{2,1,0:T(8,128)} custom-call(s32[2]{0:T(128)} %owners_ref.1, bf16[2,512,96]{2,1,0:T(8,128)(2,1)} %get-tuple-element.21.tail_ref, bf16[2,16,96]{2,1,0:T(8,128)(2,1)} %get-tuple-element.22.end_ref, bf16[2,256,512]{2,1,0:T(8,128)(2,1)} %get-tuple-element.18.b_ref, f32[4,256]{1,0:T(4,128)} %copy-done.2, f32[4,256]{1,0:T(4,128)} %copy-done.3, ...), custom_call_target="tpu_custom_call" | custom-call | tf_op jit(solution)/shard_map/block_states/pallas_call | solution.py:331
  14.5 56.8 %all_to_all.15.in_ref = f32[16,536,128]{2,1,0:T(8,128)} all-to-all(f32[16,536,128]{2,1,0:T(8,128)} %block_states.1), channel_id=1, replica_groups=mesh['seq'=16,'tp'=8,'rep'=2] {'seq'}, dimensions={0} | all-to-all | bytes 8781824 | tf_op jit(solution)/shard_map/all_to_all | solution.py:350
  71.3 5.0 %prefix_states.1 = f32[16,520,128]{2,1,0:T(8,128)} custom-call(f32[16,536,128]{2,1,0:T(8,128)} %all_to_all.15.in_ref), custom_call_target="tpu_custom_call" | custom-call | tf_op jit(solution)/shard_map/prefix_states/pallas_call | solution.py:354
  76.3 8.4 %all-to-all-start.1 = ((f32[16,520,128]{2,1,0:T(8,128)}), f32[16,520,128]{2,1,0:T(8,128)}, u32[]{:S(2)}, u32[]{:S(2)}) async-start(f32[16,520,128]{2,1,0:T(8,128)} %prefix_states.1), calls=%async_computation.1 | async-start | bytes 8519680 | tf_op jit(solution)/shard_map/all_to_all | solution.py:370
  84.8 0.1 fusion
  85.0 0.6 pad.5.factor_ref
  85.6 1.2 fusion.4
  86.8 18.5 %inner_terms.1 = (bf16[2,512,2048]{2,1,0:T(8,128)(2,1)}, bf16[2,512,96]{2,1,0:T(8,128)(2,1)}) custom-call(s32[2]{0:T(128)} %lengths_ref.3, f32[2,32,512]{2,1,0:T(8,128)} %get-tuple-element.17.run_ref, f32[2,32,512]{2,1,0:T(8,128)} %bitcast.28, bf16[2,256,512]{2,1,0:T(8,128)(2,1)} %get-tuple-element.18.b_ref, bf16[2,512,256]{2,1,0:T(8,128)(2,1)} %get-tuple-element.19.c_ref, ...), custom_call_target="tpu_custom_call" | custom-call | flops 20000000000 | bytes 33554432 | tf_op jit(solution)/shard_map/inner_terms/pallas_call | solution.py:372
  105.3 40.0 %all-to-all-done.1.held_ref = f32[16,520,128]{2,1,0:T(8,128)} async-done(((f32[16,520,128]{2,1,0:T(8,128)}), f32[16,520,128]{2,1,0:T(8,128)}, u32[]{:S(2)}, u32[]{:S(2)}) %all-to-all-start.1) | async-done | bytes 4259872 | tf_op jit(solution)/shard_map/all_to_all | solution.py:370
  145.2 1.5 slice_bitcast_fusion
  146.8 0.7 concatenate.6
  147.5 0.1 collective-permute-start.1
  147.6 8.1 %outer_terms.1 = (bf16[2,512,2048]{2,1,0:T(8,128)(2,1)}, f32[2,8,512]{2,1,0:T(8,128)}) custom-call(bf16[2,512,96]{2,1,0:T(8,128)(2,1)} %get-tuple-element.20.grow_ref, bf16[2,512,256]{2,1,0:T(8,128)(2,1)} %get-tuple-element.19.c_ref, f32[16,520,128]{2,1,0:T(8,128)} %all-to-all-done.1.held_ref, bf16[2,512,2048]{2,1,0:T(8,128)(2,1)} %get-tuple-element.24.inner_ref), custom_call_target="tpu_custom_call" | custom-call | flops 4000000000 | bytes 12582912 | tf_op jit(solution)/shard_map/outer_terms/pallas_call | solution.py:404
  155.7 0.6 copy-done.1
  156.3 1.9 %decode.1 = (f32[4,2048]{1,0:T(4,128)}, f32[8,12,128]{2,1,0:T(8,128)}) custom-call(f32[2,8,512]{2,1,0:T(8,128)} %get-tuple-element.25.square_ref, f32[2]{0:T(128)} %get-tuple-element.33.mine_ref, f32[8,2048]{1,0:T(8,128)} %get-tuple-element.36.own_ref, f32[8,2048]{1,0:T(8,128)} %copy-done.1, f32[24,32]{1,0:T(8,128)} %pad.5.factor_ref, bf16[4,2048]{1,0:T(4,128)(2,1)} %bitcast.29), custom_call_target="tpu_custom_call" | custom-call | tf_op jit(solution)/shard_map/decode/pallas_call | solution.py:436
  158.3 8.3 %all-to-all-start.2 = ((f32[8,12,128]{2,1,0:T(8,128)}), f32[8,12,128]{2,1,0:T(8,128)S(1)}, u32[]{:S(2)}, u32[]{:S(2)}) async-start(f32[8,12,128]{2,1,0:T(8,128)} %get-tuple-element.27), calls=%async_computation.2 | async-start | bytes 131072 | tf_op jit(solution)/shard_map/all_to_all | solution.py:449
  166.6 1.2 slice.17
  169.0 6.0 %all-to-all-done.2.sums_ref = f32[8,12,128]{2,1,0:T(8,128)S(1)} async-done(((f32[8,12,128]{2,1,0:T(8,128)}), f32[8,12,128]{2,1,0:T(8,128)S(1)}, u32[]{:S(2)}, u32[]{:S(2)}) %all-to-all-start.2) | async-done | bytes 49184 | tf_op jit(solution)/shard_map/all_to_all | solution.py:449
  175.0 0.6 copy-done
  175.6 5.6 %normalize.1 = (bf16[2,512,2048]{2,1,0:T(8,128)(2,1)}, bf16[4,2048]{1,0:T(4,128)(2,1)}) custom-call(f32[8,12,128]{2,1,0:T(8,128)} %copy-done, f32[1,2048]{1,0:T(1,128)} %bitcast.30, f32[1]{0:T(128)} %bitcast.12.filled_ref, f32[4,2048]{1,0:T(4,128)} %get-tuple-element.28.reading_ref, bf16[2,512,2048]{2,1,0:T(8,128)(2,1)} %get-tuple-element.29.mixed_ref), custom_call_target="tpu_custom_call" | custom-call | tf_op jit(solution)/shard_map/normalize/pallas_call | solution.py:450
  (23 shorter events, 0.3 us)
Async XLA Ops:
  1.4 5.1 %copy-start.2 = (f32[4,256]{1,0:T(4,128)}, f32[4,256]{1,0:T(4,128)S(1)}, u32[]{:S(2)}) copy-start(f32[4,256]{1,0:T(4,128)S(1)} %fusion.3.query_ref) | copy-start | bytes 12292
  1.4 5.0 %collective-permute-start = (f32[4,256]{1,0:T(4,128)S(1)}, f32[4,256]{1,0:T(4,128)S(1)}, u32[]{:S(2)}, u32[]{:S(2)}) collective-permute-start(f32[4,256]{1,0:T(4,128)S(1)} %fusion.3.query_ref), channel_id=1, source_target_pairs={{0,1},{1,0},{2,3},{3,2},{4,5},{5,4},{6,7},{7,6},{8,9},{9,8},{10,11... | collective-permute-start | bytes 12296 | tf_op jit(solution)/shard_map/ppermute | solution.py:300
  6.5 0.6 copy-start.3
  76.3 8.5 %copy-start.6 = (f32[1,4,32]{2,1,0:T(4,128)S(1)}, f32[1,4,32]{2,1,0:T(4,128)}, u32[]{:S(2)}) copy-start(f32[1,4,32]{2,1,0:T(4,128)} %param.21) | copy-start | bytes 1540
  76.3 8.6 %copy-start.5 = (f32[1,4,32]{2,1,0:T(4,128)S(1)}, f32[1,4,32]{2,1,0:T(4,128)}, u32[]{:S(2)}) copy-start(f32[1,4,32]{2,1,0:T(4,128)} %param.20) | copy-start | bytes 1540
  76.3 9.3 %copy-start.4 = (s32[2]{0:T(128)S(1)}, s32[2]{0:T(128)}, u32[]{:S(2)}) copy-start(s32[2]{0:T(128)} %owners_ref.1) | copy-start | bytes 28
  76.3 68.9 %all-to-all-start.1 = ((f32[16,520,128]{2,1,0:T(8,128)}), f32[16,520,128]{2,1,0:T(8,128)}, u32[]{:S(2)}, u32[]{:S(2)}) async-start(f32[16,520,128]{2,1,0:T(8,128)} %prefix_states.1), calls=%async_computation.1 | async-start | bytes 8519680 | tf_op jit(solution)/shard_map/all_to_all | solution.py:370
  147.5 8.2 %collective-permute-start.1 = (f32[8,2048]{1,0:T(8,128)S(1)}, f32[8,2048]{1,0:T(8,128)S(1)}, u32[]{:S(2)}, u32[]{:S(2)}) collective-permute-start(f32[8,2048]{1,0:T(8,128)S(1)} %concatenate.6), channel_id=1, source_target_pairs={{0,1},{1,0},{2,3},{3,2},{4,5},{5,4},{6,7},{7,6},{8,9},{9,8},{10,11... | collective-permute-start | bytes 196616 | tf_op jit(solution)/shard_map/ppermute | solution.py:401
  155.7 0.6 copy-start.1
  158.3 16.7 %all-to-all-start.2 = ((f32[8,12,128]{2,1,0:T(8,128)}), f32[8,12,128]{2,1,0:T(8,128)S(1)}, u32[]{:S(2)}, u32[]{:S(2)}) async-start(f32[8,12,128]{2,1,0:T(8,128)} %get-tuple-element.27), calls=%async_computation.2 | async-start | bytes 131072 | tf_op jit(solution)/shard_map/all_to_all | solution.py:449
  175.0 0.6 copy-start

commit v2 on v1

v2 whole, which is shorter than its diff:
```python
import functools

import jax
import jax.numpy as jnp
from jax import lax
from jax.experimental import pallas as pl
from jax.experimental.pallas import tpu as pltpu
from jax.sharding import PartitionSpec as P

eps_norm = 1e-05
TILE = 512
SUB = 128
HIGH = lax.Precision.HIGHEST
F32 = jnp.float32
BF16 = jnp.bfloat16


def remaining(lengths_ref, row, span):
    return lengths_ref[row] - lax.axis_index("seq") * span


def params(semantics, mib):
    return pltpu.CompilerParams(dimension_semantics=semantics, vmem_limit_bytes=mib * 2**20)


def split3(value):
    first = value.astype(BF16)
    rest = value - first.astype(F32)
    second = rest.astype(BF16)
    third = (rest - second.astype(F32)).astype(BF16)
    return jnp.concatenate([first, second, third], axis=0)


def head_columns(heads, head_size, start, width):
    row = lax.broadcasted_iota(jnp.int32, (3 * heads, width), 0)
    col = lax.broadcasted_iota(jnp.int32, (3 * heads, width), 1) + start
    return (lax.rem(row, heads) == col // head_size).astype(BF16)


def spread(parts, columns):
    return lax.dot_general(parts, columns, (((0,), (0,)), ((), ())), preferred_element_type=F32)


def pre_kernel(head_size, lengths_ref, decay_in, dt_in, bc_in, x_in, out_hbm, run_ref, b_out_ref, out_ref, decay_ref, dt_ref, bc_ref, x_ref, tail_ref, end_ref, sems, x_sems, out_sems):
    rows, heads, span = decay_ref.shape
    width, states = x_ref.shape[2], bc_ref.shape[3]
    tile = width // 2

    def load(row):
        pairs = [(decay_in, decay_ref), (dt_in, dt_ref), (bc_in, bc_ref)]
        return [
            pltpu.make_async_copy(source.at[row], target.at[row], sems.at[row, k])
            for k, (source, target) in enumerate(pairs)
        ]

    def fetch(row, part):
        lanes = pl.ds(part * tile, tile)
        return pltpu.make_async_copy(x_in.at[row, :, lanes], x_ref.at[row, :, lanes], x_sems.at[row, part])

    def send(row, part):
        parts, inside = pl.ds(part * (tile // SUB), tile // SUB), pl.ds(row * states, states)
        return pltpu.make_async_copy(
            out_ref.at[parts, inside, :], out_hbm.at[parts, inside, :], out_sems.at[row, part]
        )

    def start(row):
        for copy in load(row):
            copy.start()
        for part in range(2):
            fetch(row, part).start()

    start(0)
    upto = (
        lax.broadcasted_iota(jnp.int32, (span, span), 0) <= lax.broadcasted_iota(jnp.int32, (span, span), 1)
    ).astype(BF16)
    for row in range(rows):
        for copy in load(row):
            copy.wait()
        here = lax.broadcasted_iota(jnp.int32, (heads, span), 1) < remaining(lengths_ref, row, span)
        gates = jnp.where(here, decay_ref[row], 0.0)
        rates = jnp.where(here, dt_ref[row], 0.0)
        sums = jnp.dot(split3(gates), upto, preferred_element_type=F32)
        running = sums[:heads] + sums[heads : 2 * heads] + sums[2 * heads :]
        run_ref[row] = running
        total = running[:, span - 1 : span]
        tail_ref[row] = split3(jnp.exp(total - running) * rates).T
        end_ref[row] = split3(jnp.broadcast_to(jnp.exp(total), (heads, SUB))).T[:16]
        b_out_ref[row] = bc_ref[row, :, 0, :].T
        if row + 1 < rows:
            start(row + 1)
        for part in range(2):
            columns = head_columns(heads, head_size, part * tile, tile)
            weights = jnp.dot(tail_ref[row], columns, preferred_element_type=F32)
            ends = jnp.dot(end_ref[row], columns, preferred_element_type=F32)
            fetch(row, part).wait()
            values = x_ref[row, :, part * tile : (part + 1) * tile].astype(F32)
            weighted = (values * weights).astype(BF16)
            state = jnp.dot(b_out_ref[row], weighted, preferred_element_type=F32)
            for k in range(tile // SUB):
                chunk, lanes = part * (tile // SUB) + k, slice(k * SUB, (k + 1) * SUB)
                out_ref[chunk, row * states : (row + 1) * states, :] = state[:, lanes]
                rest = slice(rows * states + 4 * row, rows * states + 4 * row + 4)
                out_ref[chunk, rest, :] = ends[:4, lanes]
            send(row, part).start()
    rest = pl.ds(rows * states, 8)
    last = pltpu.make_async_copy(out_ref.at[:, rest, :], out_hbm.at[:, rest, :], sems.at[0, 3])
    last.start()
    for row in range(rows):
        for part in range(2):
            send(row, part).wait()
    last.wait()


def keys_kernel(owners_ref, query_ref, other_ref, _, out_ref):
    half = pl.program_id(0)
    mine, other = slot_flags(owners_ref)
    chosen = [mine[p] * query_ref[...] + other[p] * other_ref[...] for p in range(2)]
    chosen = jnp.concatenate(chosen, axis=0)
    keys = jnp.where(half == 0, chosen[:, :SUB], chosen[:, SUB:])
    for chunk in range(out_ref.shape[0]):
        out_ref[chunk] = keys


def scan_kernel(in_ref, out_ref, carry_ref, key_ref, held_ref, sems):
    step = pl.program_id(0)
    count, states = in_ref.shape[0], 256

    @pl.when(step == 0)
    def _():
        carry_ref[...] = jnp.zeros_like(carry_ref)
        key_ref[...] = jnp.zeros_like(key_ref)

    for part in range(count):
        for row in range(2):
            rows = slice(row * states, (row + 1) * states)
            before = carry_ref[rows, :]
            held_ref[step * count + part, rows, :] = before
            carry_ref[rows, :] = (
                in_ref[part, 2 * states + 4 * row : 2 * states + 4 * row + 1, :] * before + in_ref[part, rows, :]
            )
        key_ref[...] += in_ref[part, 2 * states + 8 :, :]

    def send(k):
        parts = pl.ds(k * count, count)
        rows = pl.ds(0, 2 * states)
        return pltpu.make_async_copy(held_ref.at[parts, rows, :], out_ref.at[parts, rows, :], sems.at[k])

    send(step).start()

    @pl.when(step == pl.num_programs(0) - 1)
    def _():
        first, second = key_ref[:8, :], key_ref[8:, :]
        answers = []
        for row in range(2):
            upper = carry_ref[row * states : row * states + 128, :]
            lower = carry_ref[row * states + 128 : (row + 1) * states, :]
            answer = jnp.dot(first, upper, precision=HIGH, preferred_element_type=F32)
            answers.append(answer + jnp.dot(second, lower, precision=HIGH, preferred_element_type=F32))
        pick = lax.broadcasted_iota(jnp.int32, (8, 128), 0) < 4
        both = jnp.where(pick, answers[0], answers[1])
        total = held_ref.shape[0]
        for part in range(total):
            held_ref[part, 2 * states :, :] = both
        rest = pl.ds(2 * states, 8)
        last = pltpu.make_async_copy(held_ref.at[:, rest, :], out_ref.at[:, rest, :], sems.at[total // count])
        last.start()
        for k in range(total // count):
            send(k).wait()
        last.wait()


def inner_kernel(head_size, active, *refs):
    lengths_ref, run_in, dt_in, b_in, bc_in, x_in = refs[:6]
    refs = refs[6:] if active == 1 else refs[9:]
    out_ref, grow_out, c_out, run_ref, dt_ref, b_ref, bc_ref, x_buf, out_buf, grow_ref, c_ref = refs[:11]
    scores_ref, parts_ref, sems, in_sems, out_sems = refs[11:]
    rows, heads, span = run_ref.shape
    tiles = x_buf.shape[2] // TILE

    def fetch(row, tile):
        lanes = pl.ds(pl.multiple_of(tile * TILE, TILE), TILE)
        return pltpu.make_async_copy(x_in.at[row, :, lanes], x_buf.at[row, :, lanes], in_sems.at[row, tile])

    def send(row, tile):
        lanes = pl.ds(pl.multiple_of(tile * TILE, TILE), TILE)
        return pltpu.make_async_copy(out_buf.at[row, :, lanes], out_ref.at[row, :, lanes], out_sems.at[row, tile])

    def prepare(row):
        running = run_ref[row]
        here = lax.broadcasted_iota(jnp.int32, (heads, span), 1) < remaining(lengths_ref, row, span)
        rates = jnp.where(here, dt_ref[row], 0.0)
        c_ref[row] = bc_ref[row, :, 1, :]
        scores = jnp.dot(c_ref[row], b_ref[row], preferred_element_type=F32)
        causal = lax.broadcasted_iota(jnp.int32, (span, span), 0) >= lax.broadcasted_iota(
            jnp.int32, (span, span), 1
        )
        scores_ref[...] = jnp.where(causal, scores, 0.0).astype(BF16)

        def at(index):
            return running[:, index : index + 1]

        def blocks(references, start=0):
            return jnp.concatenate(
                [
                    jnp.broadcast_to(reference, (heads, SUB))
                    for reference in references
                ],
                axis=1,
            )

        middles = blocks([at(k * SUB + SUB // 2 - 1) for k in range(4)])
        near = jnp.exp(middles - running) * rates
        own = jnp.where(here, jnp.exp(running - middles), 0.0)
        ends = blocks([at(SUB - 1), at(3 * SUB - 1)])
        odd = jnp.concatenate([running[:, :SUB], running[:, 2 * SUB : 3 * SUB]], axis=1)
        odd_rates = jnp.concatenate([rates[:, :SUB], rates[:, 2 * SUB : 3 * SUB]], axis=1)
        mid = jnp.exp(ends - odd) * odd_rates
        halves = jnp.broadcast_to(at(2 * SUB - 1), (heads, 2 * SUB))
        far = jnp.exp(halves - running[:, : 2 * SUB]) * rates[:, : 2 * SUB]
        starts = blocks([at(SUB - 1), at(2 * SUB - 1), at(3 * SUB - 1)])
        other = jnp.where(here[:, SUB:], jnp.exp(running[:, SUB:] - starts), 0.0)
        gap = jnp.broadcast_to(jnp.exp(at(3 * SUB - 1) - at(2 * SUB - 1)), (heads, SUB))
        parts_ref[...] = split3(jnp.concatenate([near, own, mid, far, other, gap], axis=1)).T
        grow_ref[row] = split3(jnp.where(here, jnp.exp(running), 0.0)).T

    def one(row, tile):
        columns = head_columns(heads, head_size, tile * TILE, TILE)
        fetch(row, tile).wait()
        lanes = pl.ds(pl.multiple_of(tile * TILE, TILE), TILE)
        values = x_buf[row, :, lanes].astype(F32)

        wide = jnp.dot(parts_ref[...], columns, preferred_element_type=F32)
        near, own, mid, far, other, gap = (
            wide[low:high]
            for low, high in ((0, 512), (512, 1024), (1024, 1280), (1280, 1536), (1536, 1920), (1920, 1921))
        )

        def part(k, n=1):
            return slice(k * SUB, (k + n) * SUB)

        def apply(rows, cols, weights):
            weighted = (values[cols] * weights).astype(BF16)
            return jnp.dot(scores_ref[rows, cols], weighted, preferred_element_type=F32)

        far = apply(part(2, 2), part(0, 2), far)
        mids = [apply(part(1), part(0), mid[:SUB]), apply(part(3), part(2), mid[SUB:])]
        others = [None, mids[0], far[:SUB], mids[1] + gap * far[SUB:]]
        for k in range(4):
            result = own[part(k)] * apply(part(k), part(k), near[part(k)])
            if others[k] is not None:
                result = result + other[part(k - 1)] * others[k]
            out_buf[row, part(k), lanes] = result.astype(BF16)
        send(row, tile).start()

    @pl.when(lax.axis_index("rep") == active)
    def _():
        loads = [
            pltpu.make_async_copy(source, target, sems.at[k])
            for k, (source, target) in enumerate(
                [(run_in, run_ref), (dt_in, dt_ref), (b_in, b_ref), (bc_in, bc_ref)]
            )
        ]
        for load in loads:
            load.start()
        for row in range(rows):
            for tile in range(tiles):
                fetch(row, tile).start()
        for load in loads:
            load.wait()
        for row in range(rows):
            prepare(row)

            @pl.loop(0, tiles)
            def _(tile):
                one(row, tile)

        stores = [
            pltpu.make_async_copy(grow_ref, grow_out, sems.at[4]),
            pltpu.make_async_copy(c_ref, c_out, sems.at[5]),
        ]
        for store in stores:
            store.start()
        for row in range(rows):
            for tile in range(tiles):
                send(row, tile).wait()
        for store in stores:
            store.wait()


def post_kernel(head_size, grow_ref, c_ref, held_ref, inner_ref, out_ref, square_ref, total_ref):
    row, tile = pl.program_id(0), pl.program_id(1)
    heads = grow_ref.shape[2] // 3
    width = inner_ref.shape[2]

    @pl.when(tile == 0)
    def _():
        total_ref[...] = jnp.zeros_like(total_ref)

    columns = head_columns(heads, head_size, tile * width, width)
    held = jnp.concatenate([held_ref[k].astype(BF16) for k in range(held_ref.shape[0])], axis=1)
    outer = jnp.dot(c_ref[0], held, preferred_element_type=F32)
    grow = jnp.dot(grow_ref[0], columns, preferred_element_type=F32)
    mixed = inner_ref[0].astype(F32) + grow * outer
    out_ref[0] = mixed.astype(BF16)
    squares = mixed * mixed
    partial = total_ref[...]
    for k in range(width // SUB):
        partial += squares[:, k * SUB : (k + 1) * SUB]
    total_ref[...] = partial

    @pl.when(tile == pl.num_programs(1) - 1)
    def _():
        square_ref[0] = lax.dot_general(
            jnp.ones((8, SUB), F32),
            partial,
            (((1,), (1,)), ((), ())),
            precision=HIGH,
            preferred_element_type=F32,
        )


def slot_flags(owners_ref):
    chip, rep = lax.axis_index("seq") * 2, lax.axis_index("rep")
    mine = [jnp.where(owners_ref[prompt] == chip + rep, 1.0, 0.0) for prompt in range(2)]
    other = [jnp.where(owners_ref[prompt] == chip + 1 - rep, 1.0, 0.0) for prompt in range(2)]
    return mine, other


def answer_kernel(owners_ref, held_ref, own_ref, sent_ref):
    mine, other = slot_flags(owners_ref)
    steps = 4
    for ref, flags in ((own_ref, mine), (sent_ref, other)):
        for chunk in range(held_ref.shape[0]):
            lanes = slice(chunk * SUB, (chunk + 1) * SUB)
            ref[:steps, lanes] = flags[0] * held_ref[chunk, :steps] + flags[1] * held_ref[chunk, steps:]
        ref[steps:, :] = jnp.full((8 - steps, ref.shape[1]), flags[0] + flags[1], F32)


def decode_kernel(head_size, square_ref, own_ref, got_ref, x_ref, key_ref, query_ref, dt_ref, decay_ref, reading_ref, sums_ref):
    steps, width = x_ref.shape
    heads = dt_ref.shape[1]
    columns = head_columns(heads, head_size, 0, width)
    products = lax.dot_general(
        key_ref[...], query_ref[...], (((1,), (1,)), ((), ())), preferred_element_type=F32
    )
    factors, where = [], {}
    for k in range(steps):
        gone = jnp.zeros((1, heads), F32)
        for j in range(k, -1, -1):
            where[j, k] = len(factors)
            factors.append(jnp.exp(gone) * dt_ref[j : j + 1, :] * products[j : j + 1, k : k + 1])
            gone = gone + decay_ref[j : j + 1, :]
        where[-1, k] = len(factors)
        factors.append(jnp.exp(gone))
    while len(factors) % 8:
        factors.append(jnp.zeros((1, heads), F32))
    factors = spread(split3(jnp.concatenate(factors, axis=0).T), columns)
    start = own_ref[...] + got_ref[...]
    values = x_ref[...].astype(F32)
    readings = []
    for k in range(steps):
        reading = factors[where[-1, k] : where[-1, k] + 1] * start[k : k + 1]
        for j in range(k + 1):
            reading = reading + factors[where[j, k] : where[j, k] + 1] * values[j : j + 1]
        readings.append(reading)
    readings = jnp.concatenate(readings, axis=0)
    filled = start[steps : steps + 1]
    reading_ref[...] = readings * filled
    squares = jnp.broadcast_to(jnp.sum(readings * readings, axis=1, keepdims=True), (steps, SUB))
    blocks = square_ref.shape[2] // SUB
    for part in range(sums_ref.shape[0]):
        for row in range(2):
            for k in range(blocks):
                line = row * blocks + k
                sums_ref[part, line : line + 1, :] = square_ref[row, :1, k * SUB : (k + 1) * SUB]
        sums_ref[part, 2 * blocks :, :] = squares


def final_kernel(channels, sums_ref, gain_ref, reading_ref, mixed_ref, out_ref, step_ref):
    row = pl.program_id(0)
    sums = jnp.sum(sums_ref[...], axis=0)
    scales = lax.rsqrt(sums / channels + eps_norm)
    gain = gain_ref[...]
    count = mixed_ref.shape[1] // SUB
    mine = jnp.where(row == 0, scales[:count], scales[count : 2 * count])
    columns = jnp.concatenate([mine, mine], axis=0).T
    for k in range(count):
        rows = slice(k * SUB, (k + 1) * SUB)
        out_ref[0, rows, :] = (mixed_ref[0, rows, :].astype(F32) * columns[:, k : k + 1] * gain).astype(BF16)

    @pl.when(row == 0)
    def _():
        step_ref[...] = (reading_ref[...] * scales[2 * count :, :1] * gain).astype(BF16)


def after(value, *others):
    return lax.optimization_barrier((value,) + others)[0]


def local(prompt_x, prompt_bc, prompt_dt, prompt_decay, lengths, owners, gain, step_x, step_bc, step_dt, step_decay):
    rows, span, heads = prompt_dt.shape
    width = prompt_x.shape[2]
    head_size = width // heads
    states = prompt_bc.shape[4]
    steps = step_x.shape[1]
    channels = width * lax.axis_size("tp")
    seq_count = lax.axis_size("seq")
    decay_t = jnp.swapaxes(prompt_decay, 1, 2)
    dt_t = jnp.swapaxes(prompt_dt, 1, 2)
    smem = pl.BlockSpec(memory_space=pltpu.SMEM)

    queries = step_bc[0, :, 1, 0].astype(F32)
    swap = [(0, 1), (1, 0)]
    other_queries = lax.ppermute(queries, "rep", swap)
    key_rows = 2 * rows * steps
    sent_rows = rows * states + 8 + key_rows
    bc = jnp.swapaxes(prompt_bc, 2, 3)[:, :, 0]
    whole = lambda *dims: pl.BlockSpec(dims, lambda *_: (0,) * len(dims))
    anywhere = pl.BlockSpec(memory_space=pl.ANY)
    hbm = pl.BlockSpec(memory_space=pltpu.HBM)
    shape = jax.ShapeDtypeStruct

    vmem = pl.BlockSpec(memory_space=pltpu.VMEM)
    chunks = width // SUB
    sent, running, b_rows = pl.pallas_call(
        functools.partial(pre_kernel, head_size),
        in_specs=[smem] + [hbm] * 4,
        out_specs=[anywhere, vmem, vmem],
        out_shape=[
            shape((chunks, sent_rows, SUB), F32),
            shape((rows, heads, span), F32),
            shape((rows, states, span), BF16),
        ],
        scratch_shapes=[
            pltpu.VMEM((chunks, sent_rows, SUB), F32),
            pltpu.VMEM((rows, heads, span), F32),
            pltpu.VMEM((rows, heads, span), F32),
            pltpu.VMEM((rows, span, 2, states), BF16),
            pltpu.VMEM((rows, span, width), BF16),
            pltpu.VMEM((rows, span, 3 * heads), BF16),
            pltpu.VMEM((rows, 16, 3 * heads), BF16),
            pltpu.SemaphoreType.DMA((rows, 4)),
            pltpu.SemaphoreType.DMA((rows, 2)),
            pltpu.SemaphoreType.DMA((rows, 2)),
        ],
        compiler_params=params(None, 58),
        name="block_states",
    )(lengths, decay_t, dt_t, bc, prompt_x)

    def inner_terms(active, begin, results):
        return pl.pallas_call(
            functools.partial(inner_kernel, head_size, active),
            in_specs=[smem] + [anywhere] * 2 + [anywhere] + [hbm] * (2 + len(results)),
            out_specs=[hbm] * 3,
            out_shape=[
                shape((rows, span, width), BF16),
                shape((rows, span, 3 * heads), BF16),
                shape((rows, span, states), BF16),
            ],
            scratch_shapes=[
                pltpu.VMEM((rows, heads, span), F32),
                pltpu.VMEM((rows, heads, span), F32),
                pltpu.VMEM((rows, states, span), BF16),
                pltpu.VMEM((rows, span, 2, states), BF16),
                pltpu.VMEM((rows, span, width), BF16),
                pltpu.VMEM((rows, span, width), BF16),
                pltpu.VMEM((rows, span, 3 * heads), BF16),
                pltpu.VMEM((rows, span, states), BF16),
                pltpu.VMEM((span, span), BF16),
            ]
            + [
                pltpu.VMEM((4 * span, 3 * heads), BF16),
                pltpu.SemaphoreType.DMA((6,)),
                pltpu.SemaphoreType.DMA((rows, width // TILE)),
                pltpu.SemaphoreType.DMA((rows, width // TILE)),
            ],
            input_output_aliases={6 + k: k for k in range(len(results))},
            compiler_params=params(None, 58 if active else 28),
            name="inner_terms",
        )(begin, running, dt_t, b_rows, bc, prompt_x, *results)

    first = inner_terms(1, lengths, [])
    sent = pl.pallas_call(
        keys_kernel,
        grid=(2,),
        in_specs=[smem, whole(steps, states), whole(steps, states), anywhere],
        out_specs=pl.BlockSpec((chunks, 8, SUB), lambda k: (0, rows * states // 8 + 1 + k, 0)),
        out_shape=shape(sent.shape, F32),
        input_output_aliases={3: 0},
        compiler_params=params(("arbitrary",), 60),
        name="keys",
    )(owners, queries, other_queries, after(sent, *first))

    got = lax.all_to_all(sent, "seq", 0, 0)

    per_step = 8
    back_rows = rows * states + 8
    back = pl.pallas_call(
        scan_kernel,
        grid=(seq_count // per_step,),
        in_specs=[pl.BlockSpec((per_step, sent_rows, SUB), lambda k: (k, 0, 0))],
        out_specs=pl.BlockSpec(memory_space=pl.ANY),
        out_shape=jax.ShapeDtypeStruct((seq_count, back_rows, SUB), F32),
        scratch_shapes=[
            pltpu.VMEM((rows * states, SUB), F32),
            pltpu.VMEM((key_rows, SUB), F32),
            pltpu.VMEM((seq_count, back_rows, SUB), F32),
            pltpu.SemaphoreType.DMA((seq_count // per_step + 1,)),
        ],
        compiler_params=params(("arbitrary",), 16),
        name="prefix_states",
    )(got)

    held = lax.all_to_all(back, "seq", 0, 0)

    own_answer, sent_answer = pl.pallas_call(
        answer_kernel,
        grid=(1,),
        in_specs=[smem, pl.BlockSpec((chunks, 8, SUB), lambda k: (0, rows * states // 8, 0))],
        out_specs=[whole(8, width)] * 2,
        out_shape=[shape((8, width), F32)] * 2,
        compiler_params=params(("arbitrary",), 4),
        name="answers",
    )(owners, held)
    inner, grows, c_rows = inner_terms(0, after(lengths, sent_answer), first)
    got_answer = lax.ppermute(after(sent_answer, inner), "rep", swap)

    big = 1024
    mixed, squares = pl.pallas_call(
        functools.partial(post_kernel, head_size),
        grid=(rows, width // big),
        in_specs=[
            pl.BlockSpec((1, span, 3 * heads), lambda r, j: (r, 0, 0)),
            pl.BlockSpec((1, span, states), lambda r, j: (r, 0, 0)),
            pl.BlockSpec((big // SUB, states, SUB), lambda r, j: (j, r, 0)),
            pl.BlockSpec((1, span, big), lambda r, j: (r, 0, j)),
        ],
        out_specs=[
            pl.BlockSpec((1, span, big), lambda r, j: (r, 0, j)),
            pl.BlockSpec((1, 8, span), lambda r, j: (r, 0, 0)),
        ],
        out_shape=[
            shape((rows, span, width), BF16),
            shape((rows, 8, span), F32),
        ],
        scratch_shapes=[pltpu.VMEM((span, SUB), F32)],
        compiler_params=params(("arbitrary", "arbitrary"), 28),
        name="outer_terms",
    )(grows, c_rows, held, inner)

    tp_count = lax.axis_size("tp")
    readings, partial = pl.pallas_call(
        functools.partial(decode_kernel, head_size),
        in_specs=[vmem] * 8,
        out_shape=[shape((steps, width), F32), shape((tp_count, rows * span // SUB + steps, SUB), F32)],
        compiler_params=params(None, 8),
        name="decode",
    )(
        squares,
        own_answer,
        got_answer,
        step_x[0],
        step_bc[0, :, 0, 0],
        step_bc[0, :, 1, 0],
        step_dt[0],
        step_decay[0],
    )
    gathered = lax.all_to_all(partial, "tp", 0, 0)
    prefill_out, decode_out = pl.pallas_call(
        functools.partial(final_kernel, float(channels)),
        grid=(rows,),
        in_specs=[
            whole(*gathered.shape),
            whole(1, width),
            whole(steps, width),
            pl.BlockSpec((1, span, width), lambda r: (r, 0, 0)),
        ],
        out_specs=[pl.BlockSpec((1, span, width), lambda r: (r, 0, 0)), whole(steps, width)],
        out_shape=[shape((rows, span, width), BF16), shape((steps, width), BF16)],
        compiler_params=params(("arbitrary",), 20),
        name="normalize",
    )(gathered, gain[None], readings, mixed)
    return (prefill_out, decode_out[None])


def solution(mesh):
    in_specs = (
        P("rep", "seq", "tp"),
        P("rep", "seq", None, "tp", None),
        P("rep", "seq", "tp"),
        P("rep", "seq", "tp"),
        P("rep"),
        P("rep"),
        P("tp"),
        P(("seq", "rep"), None, "tp"),
        P(("seq", "rep"), None, None, "tp", None),
        P(("seq", "rep"), None, "tp"),
        P(("seq", "rep"), None, "tp"),
    )
    out_specs = (P("rep", "seq", "tp"), P(("seq", "rep"), None, "tp"))
    return jax.shard_map(local, mesh=mesh, in_specs=in_specs, out_specs=out_specs, check_vma=False)
```

time: 182 us -> 150 us (0.82)
  the two profiles are of different devices: /device:TPU:28 before, /device:TPU:2 now
where the time goes in v2:
time: 150 us; the launch traced here: 149 us
  blocking collectives  111 us (74%)
  Pallas kernels  33.7 us (22%)
  local copies, waits for them, and re-layouts  2.97 us (2%)
    all_to_all x1, blocking collectives, local(): got = lax.all_to_all(sent, 'seq', 0, 0)  47.4 us
    all_to_all x1, blocking collectives, local(): held = lax.all_to_all(back, 'seq', 0, 0)  46.8 us
    all_to_all x1, blocking collectives, local(): gathered = lax.all_to_all(partial, 'tp', 0, 0)  16.6 us
    pallas_call x2, Pallas kernels, inner_terms(): pl.pallas_call(functools.partial(inner_kernel, head_size, active), in_spe...  13.1 us
    pallas_call x1, Pallas kernels, local(): pl.pallas_call(functools.partial(pre_kernel, head_size), in_specs=[smem]...  8.98 us
    pallas_call x1, Pallas kernels, local(): pl.pallas_call(functools.partial(post_kernel, head_size), grid=(rows, wid...  4.98 us
  transfers between devices with their start and end apart: 2, of which 0 were waited for; matrix products, arithmetic and copies ran while one was open for 0% of the time, Pallas kernels for 10%

profile of v2, /device:TPU:2, one launch (start us, length us, event | category | flops | bytes accessed | tf_op | source)
XLA Modules:
  0.0 148.6 jit_solution(15171951753709340495)
XLA Ops:
  0.6 0.8 fusion.1
  1.4 0.0 copy-start.14
  1.4 0.1 collective-permute-start
  1.5 9.0 %block_states.1 = (f32[16,536,128]{2,1,0:T(8,128)}, f32[2,32,512]{2,1,0:T(8,128)}, bf16[2,256,512]{2,1,0:T(8,128)(2,1)}) custom-call(s32[2]{0:T(128)} %refs_0_.2, f32[2,32,512]{2,1,0:T(8,128)} %bitcast.25, f32[2,32,512]{2,1,0:T(8,128)} %bitcast.17, bf16[2,512,2,256]{3,2,1,0:T(2,128)(2,1)} %bitcast.14, bf16[2,512,2048]{2,1,0:T(8,128)(2,1)} %refs_5_.3), custom_call_target="tpu_custom_call" | custom-call | tf_op jit(solution)/shard_map/block_states/pallas_call | solution.py:425
  10.5 0.9 inner_terms.2
  11.4 0.6 copy-done.15
  12.0 1.4 keys.1
  13.4 47.4 %all_to_all.15.in_ref = f32[16,536,128]{2,1,0:T(8,128)S(1)} all-to-all(f32[16,536,128]{2,1,0:T(8,128)} %keys.1), channel_id=1, replica_groups=mesh['seq'=16,'tp'=8,'rep'=2] {'seq'}, dimensions={0} | all-to-all | bytes 8781824 | tf_op jit(solution)/shard_map/all_to_all | solution.py:494
  60.8 1.3 prefix_states.1
  62.1 0.0 copy-start.13
  62.1 0.0 copy-start.1
  62.1 0.0 copy-start.2
  62.2 0.0 copy-start.5
  62.2 46.8 %all_to_all.16.held_ref = f32[16,520,128]{2,1,0:T(8,128)S(1)} all-to-all(f32[16,520,128]{2,1,0:T(8,128)S(1)} %prefix_states.1), channel_id=1, replica_groups=mesh['seq'=16,'tp'=8,'rep'=2] {'seq'}, dimensions={0} | all-to-all | bytes 8519680 | tf_op jit(solution)/shard_map/all_to_all | solution.py:514
  109.0 0.6 answers.1
  109.7 1.5 %copy-done = bf16[2,512,2048]{2,1,0:T(8,128)(2,1)S(1)} copy-done((bf16[2,512,2048]{2,1,0:T(8,128)(2,1)S(1)}, bf16[2,512,2048]{2,1,0:T(8,128)(2,1)}, u32[]{:S(2)}) %copy-start) | copy-done | bytes 4194328
  111.2 12.2 %inner_terms.3 = (bf16[2,512,2048]{2,1,0:T(8,128)(2,1)S(1)}, bf16[2,512,96]{2,1,0:T(8,128)(2,1)S(1)}, bf16[2,512,256]{2,1,0:T(8,128)(2,1)S(1)}) custom-call(s32[2]{0:T(128)S(1)} %copy-done.10, f32[2,32,512]{2,1,0:T(8,128)S(1)} %copy-done.7, f32[2,32,512]{2,1,0:T(8,128)S(1)} %bitcast.19, ...), custom_call_target="tpu_custom_call", output_to_operand_aliasing={{0}: (6, {}), {1}: (7, {}), {2}: (8, {})} | custom-call | tf_op jit(solution)/shard_map/inner_terms/pallas_call | solution.py:451
  123.4 0.1 collective-permute-start.1
  123.6 0.0 copy-start.11
  123.6 0.0 copy-start.12
  123.6 5.0 %outer_terms.1 = (bf16[2,512,2048]{2,1,0:T(8,128)(2,1)S(1)}, f32[2,8,512]{2,1,0:T(8,128)S(1)}) custom-call(bf16[2,512,96]{2,1,0:T(8,128)(2,1)S(1)} %get-tuple-element.31.grow_ref, bf16[2,512,256]{2,1,0:T(8,128)(2,1)S(1)} %get-tuple-element.32.c_ref, f32[16,520,128]{2,1,0:T(8,128)S(1)} %all_to_all.16.held_ref, ...), custom_call_target="tpu_custom_call" | custom-call | tf_op jit(solution)/shard_map/outer_terms/pallas_call | solution.py:529
  128.6 0.6 decode.1
  129.2 16.6 %all_to_all.17.sums_ref = f32[8,12,128]{2,1,0:T(8,128)S(1)} all-to-all(f32[8,12,128]{2,1,0:T(8,128)S(1)} %get-tuple-element.37), channel_id=1, replica_groups=mesh['seq'=16,'tp'=8,'rep'=2] {'tp'}, dimensions={0} | all-to-all | bytes 98304 | tf_op jit(solution)/shard_map/all_to_all | solution.py:568
  145.9 2.7 %normalize.1 = (bf16[2,512,2048]{2,1,0:T(8,128)(2,1)}, bf16[4,2048]{1,0:T(4,128)(2,1)}) custom-call(f32[8,12,128]{2,1,0:T(8,128)S(1)} %all_to_all.17.sums_ref, f32[1,2048]{1,0:T(1,128)S(1)} %bitcast.21, f32[4,2048]{1,0:T(4,128)S(1)} %get-tuple-element.38.reading_ref, bf16[2,512,2048]{2,1,0:T(8,128)(2,1)S(1)} %get-tuple-element.39.mixed_ref), custom_call_target="tpu_custom_call" | custom-call | tf_op jit(solution)/shard_map/normalize/pallas_call | solution.py:569
  (27 shorter events, 0.1 us)
Async XLA Ops:
  1.4 10.0 %copy-start.14 = (f32[4,256]{1,0:T(4,128)}, f32[4,256]{1,0:T(4,128)S(1)}, u32[]{:S(2)}) copy-start(f32[4,256]{1,0:T(4,128)S(1)} %get-tuple-element.42.query_ref) | copy-start | bytes 12292
  1.4 10.0 %collective-permute-start = (f32[4,256]{1,0:T(4,128)S(1)}, f32[4,256]{1,0:T(4,128)S(1)}, u32[]{:S(2)}, u32[]{:S(2)}) collective-permute-start(f32[4,256]{1,0:T(4,128)S(1)} %get-tuple-element.42.query_ref), channel_id=1, source_target_pairs={{0,1},{1,0},{2,3},{3,2},{4,5},{5,4},{6,7},{7,6},{8,9},{9,8},{10,11... | collective-permute-start | bytes 12296 | tf_op jit(solution)/shard_map/ppermute | solution.py:414
  11.4 0.6 copy-start.15
  62.1 46.9 %copy-start.13 = (s32[2]{0:T(128)S(1)}, s32[2]{0:T(128)}, u32[]{:S(2)}) copy-start(s32[2]{0:T(128)} %owners_ref.3) | copy-start | bytes 28
  62.1 47.5 %copy-start.1 = (bf16[2,512,2048]{2,1,0:T(8,128)(2,1)S(1)}, bf16[2,512,2048]{2,1,0:T(8,128)(2,1)}, u32[]{:S(2)}) copy-start(bf16[2,512,2048]{2,1,0:T(8,128)(2,1)} %get-tuple-element.25.refs_6_) | copy-start | bytes 12582916
  62.1 47.5 %copy-start.2 = (bf16[2,512,2,1,256]{4,2,3,1,0:T(2,128)(2,1)S(1)}, bf16[2,512,2,1,256]{4,2,3,1,0:T(2,128)(2,1)}, u32[]{:S(2)}) copy-start(bf16[2,512,2,1,256]{4,2,3,1,0:T(2,128)(2,1)} %param.12) | copy-start | bytes 3145732
  62.1 47.5 %copy-start.3 = (bf16[2,256,512]{2,1,0:T(8,128)(2,1)S(1)}, bf16[2,256,512]{2,1,0:T(8,128)(2,1)}, u32[]{:S(2)}) copy-start(bf16[2,256,512]{2,1,0:T(8,128)(2,1)} %get-tuple-element.24.refs_3_) | copy-start | bytes 1572868
  62.2 47.5 %copy-start.4 = (bf16[2,512,256]{2,1,0:T(8,128)(2,1)S(1)}, bf16[2,512,256]{2,1,0:T(8,128)(2,1)}, u32[]{:S(2)}) copy-start(bf16[2,512,256]{2,1,0:T(8,128)(2,1)} %get-tuple-element.27.refs_8_) | copy-start | bytes 1572868
  62.2 47.5 %copy-start.5 = (f32[2,512,32]{1,2,0:T(8,128)S(1)}, f32[2,512,32]{1,2,0:T(8,128)}, u32[]{:S(2)}) copy-start(f32[2,512,32]{1,2,0:T(8,128)} %param.13) | copy-start | bytes 393220
  62.2 47.5 %copy-start.6 = (bf16[2,512,96]{2,1,0:T(8,128)(2,1)S(1)}, bf16[2,512,96]{2,1,0:T(8,128)(2,1)}, u32[]{:S(2)}) copy-start(bf16[2,512,96]{2,1,0:T(8,128)(2,1)} %get-tuple-element.26.refs_7_) | copy-start | bytes 589828
  62.2 47.5 %copy-start.7 = (f32[2,32,512]{2,1,0:T(8,128)S(1)}, f32[2,32,512]{2,1,0:T(8,128)}, u32[]{:S(2)}) copy-start(f32[2,32,512]{2,1,0:T(8,128)} %get-tuple-element.23.refs_1_) | copy-start | bytes 393220
  109.0 2.2 %copy-start = (bf16[2,512,2048]{2,1,0:T(8,128)(2,1)S(1)}, bf16[2,512,2048]{2,1,0:T(8,128)(2,1)}, u32[]{:S(2)}) copy-start(bf16[2,512,2048]{2,1,0:T(8,128)(2,1)} %refs_5_.3) | copy-start | bytes 12582916
  109.0 2.2 %copy-start.10 = (s32[2]{0:T(128)S(1)}, s32[2]{0:T(128)}, u32[]{:S(2)}) copy-start(s32[2]{0:T(128)} %refs_0_.2) | copy-start | bytes 28
  123.4 5.1 %collective-permute-start.1 = (f32[8,2048]{1,0:T(8,128)S(1)}, f32[8,2048]{1,0:T(8,128)S(1)}, u32[]{:S(2)}, u32[]{:S(2)}) collective-permute-start(f32[8,2048]{1,0:T(8,128)S(1)} %get-tuple-element.36), channel_id=1, source_target_pairs={{0,1},{1,0},{2,3},{3,2},{4,5},{5,4},{6,7},{7,6},{8,9},{9,8},{10,11... | collective-permute-start | bytes 196616 | tf_op jit(solution)/shard_map/ppermute | solution.py:526
  123.5 5.0 %copy-start.8 = (bf16[1,4,2048]{2,1,0:T(4,128)(2,1)S(1)}, bf16[1,4,2048]{2,1,0:T(4,128)(2,1)}, u32[]{:S(2)}) copy-start(bf16[1,4,2048]{2,1,0:T(4,128)(2,1)} %param.18) | copy-start | bytes 49156
  123.6 5.0 %copy-start.11 = (f32[1,4,32]{2,1,0:T(4,128)S(1)}, f32[1,4,32]{2,1,0:T(4,128)}, u32[]{:S(2)}) copy-start(f32[1,4,32]{2,1,0:T(4,128)} %param.20) | copy-start | bytes 1540
  123.6 5.0 %copy-start.12 = (f32[1,4,32]{2,1,0:T(4,128)S(1)}, f32[1,4,32]{2,1,0:T(4,128)}, u32[]{:S(2)}) copy-start(f32[1,4,32]{2,1,0:T(4,128)} %param.21) | copy-start | bytes 1540
  123.6 22.3 %copy-start.9 = (f32[2048]{0:T(1024)S(1)}, f32[2048]{0:T(1024)}, u32[]{:S(2)}) copy-start(f32[2048]{0:T(1024)} %param.17) | copy-start | bytes 24580

commit v3 on v2

--- a/solution.py
+++ b/solution.py
@@ -8,7 +8,7 @@
 from jax.sharding import PartitionSpec as P
 
 eps_norm = 1e-05
-TILE = 512
+EARLY, LATE = 512, 2048
 SUB = 128
 HIGH = lax.Precision.HIGHEST
 F32 = jnp.float32
@@ -69,7 +69,8 @@
         for part in range(2):
             fetch(row, part).start()
 
-    start(0)
+    for row in range(rows):
+        start(row)
     upto = (
         lax.broadcasted_iota(jnp.int32, (span, span), 0) <= lax.broadcasted_iota(jnp.int32, (span, span), 1)
     ).astype(BF16)
@@ -86,8 +87,6 @@
         tail_ref[row] = split3(jnp.exp(total - running) * rates).T
         end_ref[row] = split3(jnp.broadcast_to(jnp.exp(total), (heads, SUB))).T[:16]
         b_out_ref[row] = bc_ref[row, :, 0, :].T
-        if row + 1 < rows:
-            start(row + 1)
         for part in range(2):
             columns = head_columns(heads, head_size, part * tile, tile)
             weights = jnp.dot(tail_ref[row], columns, preferred_element_type=F32)
@@ -111,16 +110,6 @@
     last.wait()
 
 
-def keys_kernel(owners_ref, query_ref, other_ref, _, out_ref):
-    half = pl.program_id(0)
-    mine, other = slot_flags(owners_ref)
-    chosen = [mine[p] * query_ref[...] + other[p] * other_ref[...] for p in range(2)]
-    chosen = jnp.concatenate(chosen, axis=0)
-    keys = jnp.where(half == 0, chosen[:, :SUB], chosen[:, SUB:])
-    for chunk in range(out_ref.shape[0]):
-        out_ref[chunk] = keys
-
-
 def scan_kernel(in_ref, out_ref, carry_ref, key_ref, held_ref, sems):
     step = pl.program_id(0)
     count, states = in_ref.shape[0], 256
@@ -169,20 +158,35 @@
         last.wait()
 
 
-def inner_kernel(head_size, active, *refs):
+def inner_kernel(head_size, active, size, *refs):
     lengths_ref, run_in, dt_in, b_in, bc_in, x_in = refs[:6]
-    refs = refs[6:] if active == 1 else refs[9:]
-    out_ref, grow_out, c_out, run_ref, dt_ref, b_ref, bc_ref, x_buf, out_buf, grow_ref, c_ref = refs[:11]
-    scores_ref, parts_ref, sems, in_sems, out_sems = refs[11:]
+    if active == 1:
+        owners_ref, query_ref, other_ref, _, out_ref, grow_out, c_out, sent_ref, keys_buf, keys_sem = refs[6:16]
+        refs = refs[16:]
+        mine, other = slot_flags(owners_ref)
+        chosen = [mine[p] * query_ref[...] + other[p] * other_ref[...] for p in range(2)]
+        chosen = jnp.concatenate(chosen, axis=0)
+        for chunk in range(keys_buf.shape[0]):
+            keys_buf[chunk, :8, :] = chosen[:, :SUB]
+            keys_buf[chunk, 8:, :] = chosen[:, SUB:]
+        count = keys_buf.shape[1]
+        place = pl.ds(sent_ref.shape[1] - count, count)
+        keys_copy = pltpu.make_async_copy(keys_buf, sent_ref.at[:, place, :], keys_sem)
+        keys_copy.start()
+    else:
+        out_ref, grow_out, c_out = refs[9:12]
+        refs = refs[12:]
+    run_ref, dt_ref, b_ref, bc_ref, x_buf, out_buf, grow_ref, c_ref = refs[:8]
+    scores_ref, parts_ref, sems, in_sems, out_sems = refs[8:]
     rows, heads, span = run_ref.shape
-    tiles = x_buf.shape[2] // TILE
+    tiles = x_buf.shape[2] // size
 
     def fetch(row, tile):
-        lanes = pl.ds(pl.multiple_of(tile * TILE, TILE), TILE)
+        lanes = pl.ds(pl.multiple_of(tile * size, size), size)
         return pltpu.make_async_copy(x_in.at[row, :, lanes], x_buf.at[row, :, lanes], in_sems.at[row, tile])
 
     def send(row, tile):
-        lanes = pl.ds(pl.multiple_of(tile * TILE, TILE), TILE)
+        lanes = pl.ds(pl.multiple_of(tile * size, size), size)
         return pltpu.make_async_copy(out_buf.at[row, :, lanes], out_ref.at[row, :, lanes], out_sems.at[row, tile])
 
     def prepare(row):
@@ -208,48 +212,53 @@
                 axis=1,
             )
 
-        middles = blocks([at(k * SUB + SUB // 2 - 1) for k in range(4)])
+        ends = [at((k + 1) * SUB - 1) for k in range(4)]
+        halves = [at(k * SUB + SUB // 2 - 1) for k in range(4)]
+        middles = blocks(halves)
         near = jnp.exp(middles - running) * rates
         own = jnp.where(here, jnp.exp(running - middles), 0.0)
-        ends = blocks([at(SUB - 1), at(3 * SUB - 1)])
-        odd = jnp.concatenate([running[:, :SUB], running[:, 2 * SUB : 3 * SUB]], axis=1)
-        odd_rates = jnp.concatenate([rates[:, :SUB], rates[:, 2 * SUB : 3 * SUB]], axis=1)
-        mid = jnp.exp(ends - odd) * odd_rates
-        halves = jnp.broadcast_to(at(2 * SUB - 1), (heads, 2 * SUB))
-        far = jnp.exp(halves - running[:, : 2 * SUB]) * rates[:, : 2 * SUB]
-        starts = blocks([at(SUB - 1), at(2 * SUB - 1), at(3 * SUB - 1)])
-        other = jnp.where(here[:, SUB:], jnp.exp(running[:, SUB:] - starts), 0.0)
-        gap = jnp.broadcast_to(jnp.exp(at(3 * SUB - 1) - at(2 * SUB - 1)), (heads, SUB))
-        parts_ref[...] = split3(jnp.concatenate([near, own, mid, far, other, gap], axis=1)).T
+        gaps = [
+            ends[0] - halves[0],
+            ends[2] - halves[2],
+            ends[1] - halves[1],
+            ends[1] - ends[0],
+            ends[2] - ends[1],
+            halves[1] - ends[0],
+            halves[2] - ends[1],
+            halves[3] - ends[2],
+        ]
+        gaps = jnp.exp(jnp.concatenate(gaps, axis=1))
+        gaps = jnp.concatenate([gaps, jnp.zeros((heads, SUB - gaps.shape[1]), F32)], axis=1)
+        parts_ref[...] = split3(jnp.concatenate([near, own, gaps], axis=1)).T
         grow_ref[row] = split3(jnp.where(here, jnp.exp(running), 0.0)).T
 
     def one(row, tile):
-        columns = head_columns(heads, head_size, tile * TILE, TILE)
+        columns = head_columns(heads, head_size, tile * size, size)
         fetch(row, tile).wait()
-        lanes = pl.ds(pl.multiple_of(tile * TILE, TILE), TILE)
+        lanes = pl.ds(pl.multiple_of(tile * size, size), size)
         values = x_buf[row, :, lanes].astype(F32)
 
-        wide = jnp.dot(parts_ref[...], columns, preferred_element_type=F32)
-        near, own, mid, far, other, gap = (
-            wide[low:high]
-            for low, high in ((0, 512), (512, 1024), (1024, 1280), (1280, 1536), (1536, 1920), (1920, 1921))
-        )
+        wide = jnp.dot(parts_ref[: 2 * span + 16], columns, preferred_element_type=F32)
+        near, own = wide[:span], wide[span : 2 * span]
+        gap = [wide[2 * span + k : 2 * span + k + 1] for k in range(8)]
 
         def part(k, n=1):
             return slice(k * SUB, (k + n) * SUB)
 
-        def apply(rows, cols, weights):
-            weighted = (values[cols] * weights).astype(BF16)
-            return jnp.dot(scores_ref[rows, cols], weighted, preferred_element_type=F32)
-
+        def apply(rows, cols, weighted):
+            return jnp.dot(scores_ref[rows, cols], weighted.astype(BF16), preferred_element_type=F32)
+
+        weighted = values * near
+        mids = [weighted[part(0)] * gap[0], weighted[part(2)] * gap[1]]
+        far = jnp.concatenate([mids[0] * gap[3], weighted[part(1)] * gap[2]], axis=0)
         far = apply(part(2, 2), part(0, 2), far)
-        mids = [apply(part(1), part(0), mid[:SUB]), apply(part(3), part(2), mid[SUB:])]
-        others = [None, mids[0], far[:SUB], mids[1] + gap * far[SUB:]]
+        mids = [apply(part(1), part(0), mids[0]), apply(part(3), part(2), mids[1])]
+        others = [None, gap[5] * mids[0], gap[6] * far[:SUB], gap[7] * (mids[1] + gap[4] * far[SUB:])]
         for k in range(4):
-            result = own[part(k)] * apply(part(k), part(k), near[part(k)])
+            result = apply(part(k), part(k), weighted[part(k)])
             if others[k] is not None:
-                result = result + other[part(k - 1)] * others[k]
-            out_buf[row, part(k), lanes] = result.astype(BF16)
+                result = result + others[k]
+            out_buf[row, part(k), lanes] = (own[part(k)] * result).astype(BF16)
         send(row, tile).start()
 
     @pl.when(lax.axis_index("rep") == active)
@@ -285,6 +294,9 @@
                 send(row, tile).wait()
         for store in stores:
             store.wait()
+
+    if active == 1:
+        keys_copy.wait()
 
 
 def post_kernel(head_size, grow_ref, c_ref, held_ref, inner_ref, out_ref, square_ref, total_ref):
@@ -393,6 +405,14 @@
         step_ref[...] = (reading_ref[...] * scales[2 * count :, :1] * gain).astype(BF16)
 
 
+def total_over(value, axis):
+    count, bit = lax.axis_size(axis), 1
+    while bit < count:
+        value = value + lax.ppermute(value, axis, [(k, k ^ bit) for k in range(count)])
+        bit *= 2
+    return value
+
+
 def after(value, *others):
     return lax.optimization_barrier((value,) + others)[0]
 
@@ -417,14 +437,13 @@
     bc = jnp.swapaxes(prompt_bc, 2, 3)[:, :, 0]
     whole = lambda *dims: pl.BlockSpec(dims, lambda *_: (0,) * len(dims))
     anywhere = pl.BlockSpec(memory_space=pl.ANY)
-    hbm = pl.BlockSpec(memory_space=pltpu.HBM)
     shape = jax.ShapeDtypeStruct
 
     vmem = pl.BlockSpec(memory_space=pltpu.VMEM)
     chunks = width // SUB
     sent, running, b_rows = pl.pallas_call(
         functools.partial(pre_kernel, head_size),
-        in_specs=[smem] + [hbm] * 4,
+        in_specs=[smem] + [anywhere] * 4,
         out_specs=[anywhere, vmem, vmem],
         out_shape=[
             shape((chunks, sent_rows, SUB), F32),
@@ -447,17 +466,21 @@
         name="block_states",
     )(lengths, decay_t, dt_t, bc, prompt_x)
 
-    def inner_terms(active, begin, results):
+    def inner_terms(active, begin, more, results):
+        early = active == 1
+        size = EARLY if early else LATE
         return pl.pallas_call(
-            functools.partial(inner_kernel, head_size, active),
-            in_specs=[smem] + [anywhere] * 2 + [anywhere] + [hbm] * (2 + len(results)),
-            out_specs=[hbm] * 3,
+            functools.partial(inner_kernel, head_size, active, size),
+            in_specs=[smem] + [anywhere] * 5 + ([smem, vmem, vmem, anywhere] if early else [anywhere] * 3),
+            out_specs=[anywhere] * (4 if early else 3),
             out_shape=[
                 shape((rows, span, width), BF16),
                 shape((rows, span, 3 * heads), BF16),
                 shape((rows, span, states), BF16),
-            ],
-            scratch_shapes=[
+            ]
+            + [shape((chunks, sent_rows, SUB), F32)] * early,
+            scratch_shapes=[pltpu.VMEM((chunks, key_rows, SUB), F32), pltpu.SemaphoreType.DMA] * early
+            + [
                 pltpu.VMEM((rows, heads, span), F32),
                 pltpu.VMEM((rows, heads, span), F32),
                 pltpu.VMEM((rows, states, span), BF16),
@@ -467,29 +490,17 @@
                 pltpu.VMEM((rows, span, 3 * heads), BF16),
                 pltpu.VMEM((rows, span, states), BF16),
                 pltpu.VMEM((span, span), BF16),
-            ]
-            + [
-                pltpu.VMEM((4 * span, 3 * heads), BF16),
+                pltpu.VMEM((2 * span + SUB, 3 * heads), BF16),
                 pltpu.SemaphoreType.DMA((6,)),
-                pltpu.SemaphoreType.DMA((rows, width // TILE)),
-                pltpu.SemaphoreType.DMA((rows, width // TILE)),
+                pltpu.SemaphoreType.DMA((rows, width // size)),
+                pltpu.SemaphoreType.DMA((rows, width // size)),
             ],
-            input_output_aliases={6 + k: k for k in range(len(results))},
-            compiler_params=params(None, 58 if active else 28),
+            input_output_aliases={9: 3} if early else {6 + k: k for k in range(3)},
+            compiler_params=params(None, 58 if early else 40),
             name="inner_terms",
-        )(begin, running, dt_t, b_rows, bc, prompt_x, *results)
-
-    first = inner_terms(1, lengths, [])
-    sent = pl.pallas_call(
-        keys_kernel,
-        grid=(2,),
-        in_specs=[smem, whole(steps, states), whole(steps, states), anywhere],
-        out_specs=pl.BlockSpec((chunks, 8, SUB), lambda k: (0, rows * states // 8 + 1 + k, 0)),
-        out_shape=shape(sent.shape, F32),
-        input_output_aliases={3: 0},
-        compiler_params=params(("arbitrary",), 60),
-        name="keys",
-    )(owners, queries, other_queries, after(sent, *first))
+        )(begin, running, dt_t, b_rows, bc, prompt_x, *more, *results)
+
+    *first, sent = inner_terms(1, lengths, [owners, queries, other_queries, sent], [])
 
     got = lax.all_to_all(sent, "seq", 0, 0)
 
@@ -522,7 +533,7 @@
         compiler_params=params(("arbitrary",), 4),
         name="answers",
     )(owners, held)
-    inner, grows, c_rows = inner_terms(0, after(lengths, sent_answer), first)
+    inner, grows, c_rows = inner_terms(0, after(lengths, sent_answer), [], first)
     got_answer = lax.ppermute(after(sent_answer, inner), "rep", swap)
 
     big = 1024
@@ -548,11 +559,10 @@
         name="outer_terms",
     )(grows, c_rows, held, inner)
 
-    tp_count = lax.axis_size("tp")
     readings, partial = pl.pallas_call(
         functools.partial(decode_kernel, head_size),
         in_specs=[vmem] * 8,
-        out_shape=[shape((steps, width), F32), shape((tp_count, rows * span // SUB + steps, SUB), F32)],
+        out_shape=[shape((steps, width), F32), shape((1, rows * span // SUB + steps, SUB), F32)],
         compiler_params=params(None, 8),
         name="decode",
     )(
@@ -565,7 +575,7 @@
         step_dt[0],
         step_decay[0],
     )
-    gathered = lax.all_to_all(partial, "tp", 0, 0)
+    gathered = total_over(partial, "tp")
     prefill_out, decode_out = pl.pallas_call(
         functools.partial(final_kernel, float(channels)),
         grid=(rows,),

time: 150 us -> 149 us (level)
  blocking collectives: 111 us -> 96.9 us
  starting transfers between devices: 0.19 us -> 13.4 us
  waiting for transfers between devices: 0.01 us -> 4.99 us
  Pallas kernels: 33.7 us -> 29.5 us
    all_to_all x1 -> x0, blocking collectives: 16.6 us -> none  [local(): gathered = lax.all_to_all(partial, 'tp', 0, 0)]
    ppermute x0 -> x3, starting transfers between devices: none -> 12.1 us  [total_over(): lax.ppermute(value, axis, [(k, k ^ bit) for k in range(count)])]
    ppermute x0 -> x3, waiting for transfers between devices: none -> 4.99 us  [total_over(): lax.ppermute(value, axis, [(k, k ^ bit) for k in range(count)])]
    pallas_call x3 -> x2, Pallas kernels: 14.5 us -> 10.7 us  [inner_terms(): pl.pallas_call(functools.partial(inner_kernel, head_size, active, size),...]
    all_to_all x1, blocking collectives: 47.4 us -> 49.5 us  [local(): got = lax.all_to_all(sent, 'seq', 0, 0)]
  transfers between devices with their start and end apart: 2 -> 5, of which waited for: 0 -> 3; matrix products, arithmetic and copies ran while one was open for 0% -> 0% of each run, Pallas kernels for 10% -> 9%
where the time goes in v3:
time: 149 us
  blocking collectives  96.9 us (65%)
  Pallas kernels  29.5 us (20%)
  starting transfers between devices  13.4 us (9%)
  waiting for transfers between devices  4.99 us (3%)
  local copies, waits for them, and re-layouts  2.95 us (2%)
    all_to_all x1, blocking collectives, local(): got = lax.all_to_all(sent, 'seq', 0, 0)  49.5 us
    all_to_all x1, blocking collectives, local(): held = lax.all_to_all(back, 'seq', 0, 0)  47.5 us
    ppermute x3, starting transfers between devices, total_over(): lax.ppermute(value, axis, [(k, k ^ bit) for k in range(count)])  12.1 us
    pallas_call x2, Pallas kernels, inner_terms(): pl.pallas_call(functools.partial(inner_kernel, head_size, active, size),...  10.7 us
    pallas_call x1, Pallas kernels, local(): pl.pallas_call(functools.partial(pre_kernel, head_size), in_specs=[smem]...  8.63 us
    pallas_call x1, Pallas kernels, local(): pl.pallas_call(functools.partial(post_kernel, head_size), grid=(rows, wid...  5 us
    ppermute x3, waiting for transfers between devices, total_over(): lax.ppermute(value, axis, [(k, k ^ bit) for k in range(count)])  4.99 us
  transfers between devices with their start and end apart: 5, of which 3 were waited for; matrix products, arithmetic and copies ran while one was open for 0% of the time, Pallas kernels for 9%

profile of v3, /device:TPU:2, one launch (start us, length us, event | category | flops | bytes accessed | tf_op | source)
XLA Modules:
  0.0 148.6 jit_solution(13989817404011822224)
XLA Ops:
  0.6 0.8 fusion.1
  1.4 0.1 collective-permute-start
  1.5 8.6 %block_states.1 = (f32[16,536,128]{2,1,0:T(8,128)}, f32[2,32,512]{2,1,0:T(8,128)}, bf16[2,256,512]{2,1,0:T(8,128)(2,1)}) custom-call(s32[2]{0:T(128)} %refs_0_.2, f32[2,32,512]{2,1,0:T(8,128)} %bitcast.25, f32[2,32,512]{2,1,0:T(8,128)} %bitcast.17, bf16[2,512,2,256]{3,2,1,0:T(2,128)(2,1)} %bitcast.14, bf16[2,512,2048]{2,1,0:T(8,128)(2,1)} %refs_5_.3), custom_call_target="tpu_custom_call" | custom-call | tf_op jit(solution)/shard_map/block_states/pallas_call | solution.py:444
  10.2 0.6 copy-done.15
  10.8 1.6 %inner_terms.2 = (bf16[2,512,2048]{2,1,0:T(8,128)(2,1)}, bf16[2,512,96]{2,1,0:T(8,128)(2,1)}, bf16[2,512,256]{2,1,0:T(8,128)(2,1)}, f32[16,536,128]{2,1,0:T(8,128)}) custom-call(s32[2]{0:T(128)} %refs_0_.2, f32[2,32,512]{2,1,0:T(8,128)} %get-tuple-element.22.refs_1_, f32[2,32,512]{2,1,0:T(8,128)} %bitcast.18, ...), custom_call_target="tpu_custom_call", output_to_operand_aliasing={{3}: (9, {})} | custom-call | tf_op jit(solution)/shard_map/inner_terms/pallas_call | solution.py:472
  12.4 49.5 %all_to_all.10.in_ref = f32[16,536,128]{2,1,0:T(8,128)S(1)} all-to-all(f32[16,536,128]{2,1,0:T(8,128)} %get-tuple-element.25), channel_id=1, replica_groups=mesh['seq'=16,'tp'=8,'rep'=2] {'seq'}, dimensions={0} | all-to-all | bytes 8781824 | tf_op jit(solution)/shard_map/all_to_all | solution.py:505
  61.9 1.2 prefix_states.1
  63.1 0.0 copy-start.2
  63.2 0.0 copy-start.5
  63.2 47.5 %all_to_all.11.held_ref = f32[16,520,128]{2,1,0:T(8,128)S(1)} all-to-all(f32[16,520,128]{2,1,0:T(8,128)S(1)} %prefix_states.1), channel_id=1, replica_groups=mesh['seq'=16,'tp'=8,'rep'=2] {'seq'}, dimensions={0} | all-to-all | bytes 8519680 | tf_op jit(solution)/shard_map/all_to_all | solution.py:525
  110.7 0.6 answers.1
  111.3 1.5 %copy-done = bf16[2,512,2048]{2,1,0:T(8,128)(2,1)S(1)} copy-done((bf16[2,512,2048]{2,1,0:T(8,128)(2,1)S(1)}, bf16[2,512,2048]{2,1,0:T(8,128)(2,1)}, u32[]{:S(2)}) %copy-start) | copy-done | bytes 4194328
  112.8 9.0 %inner_terms.3 = (bf16[2,512,2048]{2,1,0:T(8,128)(2,1)S(1)}, bf16[2,512,96]{2,1,0:T(8,128)(2,1)S(1)}, bf16[2,512,256]{2,1,0:T(8,128)(2,1)S(1)}) custom-call(s32[2]{0:T(128)S(1)} %copy-done.10, f32[2,32,512]{2,1,0:T(8,128)S(1)} %copy-done.7, f32[2,32,512]{2,1,0:T(8,128)S(1)} %bitcast.19, ...), custom_call_target="tpu_custom_call", output_to_operand_aliasing={{0}: (6, {}), {1}: (7, {}), {2}: (8, {})} | custom-call | tf_op jit(solution)/shard_map/inner_terms/pallas_call | solution.py:472
  121.9 1.2 collective-permute-start.1
  123.2 0.0 copy-start.9
  123.2 5.0 %outer_terms.1 = (bf16[2,512,2048]{2,1,0:T(8,128)(2,1)S(1)}, f32[2,8,512]{2,1,0:T(8,128)S(1)}) custom-call(bf16[2,512,96]{2,1,0:T(8,128)(2,1)S(1)} %get-tuple-element.31.grow_ref, bf16[2,512,256]{2,1,0:T(8,128)(2,1)S(1)} %get-tuple-element.32.c_ref, f32[16,520,128]{2,1,0:T(8,128)S(1)} %all_to_all.11.held_ref, ...), custom_call_target="tpu_custom_call" | custom-call | tf_op jit(solution)/shard_map/outer_terms/pallas_call | solution.py:540
  128.2 0.6 decode.1
  128.8 1.9 %collective-permute-start.2 = (f32[1,12,128]{2,1,0:T(8,128)S(1)}, f32[1,12,128]{2,1,0:T(8,128)S(1)}, u32[]{:S(2)}, u32[]{:S(2)}) collective-permute-start(f32[1,12,128]{2,1,0:T(8,128)S(1)} %get-tuple-element.37), channel_id=1, source_target_pairs={{0,2},{2,0},{4,6},{6,4},{8,10},{10,8},{12,14},{14,12},{1,3},{3,1},... | collective-permute-start | bytes 18440 | tf_op jit(solution)/shard_map/ppermute | solution.py:411
  130.8 1.7 %collective-permute-done.2 = f32[1,12,128]{2,1,0:T(8,128)S(1)} collective-permute-done((f32[1,12,128]{2,1,0:T(8,128)S(1)}, f32[1,12,128]{2,1,0:T(8,128)S(1)}, u32[]{:S(2)}, u32[]{:S(2)}) %collective-permute-start.2) | collective-permute-done | bytes 6176 | tf_op jit(solution)/shard_map/ppermute | solution.py:411
  132.5 3.3 %collective-permute-start.3 = (f32[1,12,128]{2,1,0:T(8,128)S(1)}, f32[1,12,128]{2,1,0:T(8,128)S(1)}, u32[]{:S(2)}, u32[]{:S(2)}) collective-permute-start(f32[1,12,128]{2,1,0:T(8,128)S(1)} %add.9), channel_id=1, source_target_pairs={{0,4},{2,6},{4,0},{6,2},{8,12},{10,14},{12,8},{14,10},{1,5},{3,7},... | collective-permute-start | bytes 18440 | tf_op jit(solution)/shard_map/ppermute | solution.py:411
  135.8 1.6 %collective-permute-done.3 = f32[1,12,128]{2,1,0:T(8,128)S(1)} collective-permute-done((f32[1,12,128]{2,1,0:T(8,128)S(1)}, f32[1,12,128]{2,1,0:T(8,128)S(1)}, u32[]{:S(2)}, u32[]{:S(2)}) %collective-permute-start.3) | collective-permute-done | bytes 6176 | tf_op jit(solution)/shard_map/ppermute | solution.py:411
  137.4 6.8 %collective-permute-start.4 = (f32[1,12,128]{2,1,0:T(8,128)S(1)}, f32[1,12,128]{2,1,0:T(8,128)S(1)}, u32[]{:S(2)}, u32[]{:S(2)}) collective-permute-start(f32[1,12,128]{2,1,0:T(8,128)S(1)} %add.10), channel_id=1, source_target_pairs={{0,8},{2,10},{4,12},{6,14},{8,0},{10,2},{12,4},{14,6},{1,9},{3,11}... | collective-permute-start | bytes 18440 | tf_op jit(solution)/shard_map/ppermute | solution.py:411
  144.3 1.6 %collective-permute-done.4 = f32[1,12,128]{2,1,0:T(8,128)S(1)} collective-permute-done((f32[1,12,128]{2,1,0:T(8,128)S(1)}, f32[1,12,128]{2,1,0:T(8,128)S(1)}, u32[]{:S(2)}, u32[]{:S(2)}) %collective-permute-start.4) | collective-permute-done | bytes 6176 | tf_op jit(solution)/shard_map/ppermute | solution.py:411
  145.9 2.7 %normalize.1 = (bf16[2,512,2048]{2,1,0:T(8,128)(2,1)}, bf16[4,2048]{1,0:T(4,128)(2,1)}) custom-call(f32[1,12,128]{2,1,0:T(8,128)S(1)} %add.11.sums_ref, f32[1,2048]{1,0:T(1,128)S(1)} %bitcast.21, f32[4,2048]{1,0:T(4,128)S(1)} %get-tuple-element.38.reading_ref, bf16[2,512,2048]{2,1,0:T(8,128)(2,1)S(1)} %get-tuple-element.39.mixed_ref), custom_call_target="tpu_custom_call" | custom-call | tf_op jit(solution)/shard_map/normalize/pallas_call | solution.py:579
  (34 shorter events, 0.1 us)
Async XLA Ops:
  1.4 8.8 %copy-start.14 = (f32[4,256]{1,0:T(4,128)}, f32[4,256]{1,0:T(4,128)S(1)}, u32[]{:S(2)}) copy-start(f32[4,256]{1,0:T(4,128)S(1)} %get-tuple-element.42.refs_7_) | copy-start | bytes 12292
  1.4 8.7 %collective-permute-start = (f32[4,256]{1,0:T(4,128)S(1)}, f32[4,256]{1,0:T(4,128)S(1)}, u32[]{:S(2)}, u32[]{:S(2)}) collective-permute-start(f32[4,256]{1,0:T(4,128)S(1)} %get-tuple-element.42.refs_7_), channel_id=1, source_target_pairs={{0,1},{1,0},{2,3},{3,2},{4,5},{5,4},{6,7},{7,6},{8,9},{9,8},{10,11... | collective-permute-start | bytes 12296 | tf_op jit(solution)/shard_map/ppermute | solution.py:434
  10.2 0.6 copy-start.15
  63.1 47.5 %copy-start.13 = (s32[2]{0:T(128)S(1)}, s32[2]{0:T(128)}, u32[]{:S(2)}) copy-start(s32[2]{0:T(128)} %owners_ref.1) | copy-start | bytes 28
  63.1 48.1 %copy-start.1 = (bf16[2,512,2048]{2,1,0:T(8,128)(2,1)S(1)}, bf16[2,512,2048]{2,1,0:T(8,128)(2,1)}, u32[]{:S(2)}) copy-start(bf16[2,512,2048]{2,1,0:T(8,128)(2,1)} %get-tuple-element.28.refs_6_) | copy-start | bytes 12582916
  63.1 48.1 %copy-start.2 = (bf16[2,512,2,1,256]{4,2,3,1,0:T(2,128)(2,1)S(1)}, bf16[2,512,2,1,256]{4,2,3,1,0:T(2,128)(2,1)}, u32[]{:S(2)}) copy-start(bf16[2,512,2,1,256]{4,2,3,1,0:T(2,128)(2,1)} %param.12) | copy-start | bytes 3145732
  63.1 48.1 %copy-start.3 = (bf16[2,256,512]{2,1,0:T(8,128)(2,1)S(1)}, bf16[2,256,512]{2,1,0:T(8,128)(2,1)}, u32[]{:S(2)}) copy-start(bf16[2,256,512]{2,1,0:T(8,128)(2,1)} %get-tuple-element.23.refs_3_) | copy-start | bytes 1572868
  63.2 48.1 %copy-start.4 = (bf16[2,512,256]{2,1,0:T(8,128)(2,1)S(1)}, bf16[2,512,256]{2,1,0:T(8,128)(2,1)}, u32[]{:S(2)}) copy-start(bf16[2,512,256]{2,1,0:T(8,128)(2,1)} %get-tuple-element.30.refs_8_) | copy-start | bytes 1572868
  63.2 48.1 %copy-start.5 = (f32[2,512,32]{1,2,0:T(8,128)S(1)}, f32[2,512,32]{1,2,0:T(8,128)}, u32[]{:S(2)}) copy-start(f32[2,512,32]{1,2,0:T(8,128)} %param.13) | copy-start | bytes 393220
  63.2 48.1 %copy-start.6 = (bf16[2,512,96]{2,1,0:T(8,128)(2,1)S(1)}, bf16[2,512,96]{2,1,0:T(8,128)(2,1)}, u32[]{:S(2)}) copy-start(bf16[2,512,96]{2,1,0:T(8,128)(2,1)} %get-tuple-element.29.refs_7_) | copy-start | bytes 589828
  63.2 48.1 %copy-start.7 = (f32[2,32,512]{2,1,0:T(8,128)S(1)}, f32[2,32,512]{2,1,0:T(8,128)}, u32[]{:S(2)}) copy-start(f32[2,32,512]{2,1,0:T(8,128)} %get-tuple-element.22.refs_1_) | copy-start | bytes 393220
  110.7 2.2 %copy-start = (bf16[2,512,2048]{2,1,0:T(8,128)(2,1)S(1)}, bf16[2,512,2048]{2,1,0:T(8,128)(2,1)}, u32[]{:S(2)}) copy-start(bf16[2,512,2048]{2,1,0:T(8,128)(2,1)} %refs_5_.3) | copy-start | bytes 12582916
  110.7 2.2 %copy-start.10 = (s32[2]{0:T(128)S(1)}, s32[2]{0:T(128)}, u32[]{:S(2)}) copy-start(s32[2]{0:T(128)} %refs_0_.2) | copy-start | bytes 28
  121.9 6.3 %collective-permute-start.1 = (f32[8,2048]{1,0:T(8,128)S(1)}, f32[8,2048]{1,0:T(8,128)S(1)}, u32[]{:S(2)}, u32[]{:S(2)}) collective-permute-start(f32[8,2048]{1,0:T(8,128)S(1)} %get-tuple-element.36), channel_id=1, source_target_pairs={{0,1},{1,0},{2,3},{3,2},{4,5},{5,4},{6,7},{7,6},{8,9},{9,8},{10,11... | collective-permute-start | bytes 196616 | tf_op jit(solution)/shard_map/ppermute | solution.py:537
  123.1 5.0 %copy-start.8 = (bf16[1,4,2048]{2,1,0:T(4,128)(2,1)S(1)}, bf16[1,4,2048]{2,1,0:T(4,128)(2,1)}, u32[]{:S(2)}) copy-start(bf16[1,4,2048]{2,1,0:T(4,128)(2,1)} %param.18) | copy-start | bytes 49156
  123.1 5.1 %copy-start.11 = (f32[1,4,32]{2,1,0:T(4,128)S(1)}, f32[1,4,32]{2,1,0:T(4,128)}, u32[]{:S(2)}) copy-start(f32[1,4,32]{2,1,0:T(4,128)} %param.20) | copy-start | bytes 1540
  123.1 5.1 %copy-start.12 = (f32[1,4,32]{2,1,0:T(4,128)S(1)}, f32[1,4,32]{2,1,0:T(4,128)}, u32[]{:S(2)}) copy-start(f32[1,4,32]{2,1,0:T(4,128)} %param.21) | copy-start | bytes 1540
  123.2 22.7 %copy-start.9 = (f32[2048]{0:T(1024)S(1)}, f32[2048]{0:T(1024)}, u32[]{:S(2)}) copy-start(f32[2048]{0:T(1024)} %param.17) | copy-start | bytes 24580
  128.8 3.7 %collective-permute-start.2 = (f32[1,12,128]{2,1,0:T(8,128)S(1)}, f32[1,12,128]{2,1,0:T(8,128)S(1)}, u32[]{:S(2)}, u32[]{:S(2)}) collective-permute-start(f32[1,12,128]{2,1,0:T(8,128)S(1)} %get-tuple-element.37), channel_id=1, source_target_pairs={{0,2},{2,0},{4,6},{6,4},{8,10},{10,8},{12,14},{14,12},{1,3},{3,1},... | collective-permute-start | bytes 18440 | tf_op jit(solution)/shard_map/ppermute | solution.py:411
  132.5 4.9 %collective-permute-start.3 = (f32[1,12,128]{2,1,0:T(8,128)S(1)}, f32[1,12,128]{2,1,0:T(8,128)S(1)}, u32[]{:S(2)}, u32[]{:S(2)}) collective-permute-start(f32[1,12,128]{2,1,0:T(8,128)S(1)} %add.9), channel_id=1, source_target_pairs={{0,4},{2,6},{4,0},{6,2},{8,12},{10,14},{12,8},{14,10},{1,5},{3,7},... | collective-permute-start | bytes 18440 | tf_op jit(solution)/shard_map/ppermute | solution.py:411
  137.4 8.5 %collective-permute-start.4 = (f32[1,12,128]{2,1,0:T(8,128)S(1)}, f32[1,12,128]{2,1,0:T(8,128)S(1)}, u32[]{:S(2)}, u32[]{:S(2)}) collective-permute-start(f32[1,12,128]{2,1,0:T(8,128)S(1)} %add.10), channel_id=1, source_target_pairs={{0,8},{2,10},{4,12},{6,14},{8,0},{10,2},{12,4},{14,6},{1,9},{3,11}... | collective-permute-start | bytes 18440 | tf_op jit(solution)/shard_map/ppermute | solution.py:411
